TPU v7x, 128 devices: a whole 4x4x4 slice. The times are simulated.
128 devices in a mesh: tm: 64 (over z, y_hi, x, core), segment: 2 (over y_lo).
Axes of the slice: x: 4, y: 4 (y_hi: 2, y_lo: 2; y = y_hi * 2 + y_lo), z: 4, core: 2. Of those that a mesh axis runs over, the one named last changes fastest.
Arguments:
- tokens: bfloat16 [16384, 2560], P('tm'), may hold values from -6 to 6
- probes: int32 [2, 16384, 2560], P(None, 'tm'), may hold values from -1 to 1, as said below
- norm_gain: float32 [2560], replicated, may hold values from 0.1 to 1.9
- w_query: bfloat16 [2560, 2560], P('tm', 'segment'), may hold values from -0.125 to 0.125
- w_key: bfloat16 [2560, 2560], P('tm', 'segment'), may hold values from -0.125 to 0.125
- w_value: bfloat16 [2560, 2560], P('tm', 'segment'), may hold values from -0.125 to 0.125
- query_gain: float32 [2560], P('segment'), may hold values from 0.1 to 1.9
- key_gain: float32 [2560], P('segment'), may hold values from 0.1 to 1.9
- w_out: bfloat16 [2560, 2560], P('tm', 'segment'), may hold values from -0.125 to 0.125
Outputs:
- velocity: bfloat16 [16384, 2560], P('tm', 'segment')
- density: float32 [16384], P('tm')
Inputs may be any that keep to these rules, and one draw needn't show every extreme that they name: `probes`: each entry is -1 or 1.
All inputs are finite; a program needn't handle non-finite values.
Results may differ from a plain program's by a relative error of at most 0.013.
Values may be sent and summed in bfloat16 or wider, within the bound.
A program may use at most 128 MiB of HBM per device.

v0:
```python
import math

import jax
import jax.numpy as jnp
from jax import lax
from jax.sharding import PartitionSpec as P

HEAD_DIM = 128
WIN = 128


eps = 1e-06


def extended(block, sides, width):
    for axis, dim in sides:
        count = lax.axis_size(axis)
        forward = [(i, i + 1) for i in range(count - 1)]
        backward = [(target, source) for source, target in forward]
        low = lax.ppermute(
            lax.slice_in_dim(block, block.shape[dim] - width, None, axis=dim), axis, forward
        )
        high = lax.ppermute(lax.slice_in_dim(block, 0, width, axis=dim), axis, backward)
        block = jnp.concatenate([low, block, high], axis=dim)
    return block


def norm_pair(value, tangent, gain):
    square = jnp.mean(value * value, axis=-1, keepdims=True) + eps
    factor = lax.rsqrt(square)
    inner = jnp.mean(value * tangent, axis=-1, keepdims=True)
    return (
        value * factor * gain,
        (tangent * factor - value * (factor * factor * factor) * inner) * gain,
    )


def window_mask(query_place, key_place, total):
    offset = query_place[:, None] - key_place[None, :]
    inside = (key_place[None, :] >= 0) & (key_place[None, :] < total)
    return (offset <= WIN) & (offset >= -WIN) & inside


def attend(query, query_tan, keys, keys_tan, values, values_tan, valid):
    scale = 1.0 / math.sqrt(query.shape[-1])
    scores = jnp.einsum("qhd,khd->hqk", query, keys, preferred_element_type=jnp.float32) * scale
    weights = jnp.where(valid, jnp.exp(scores), 0.0)
    weights = weights / jnp.sum(weights, axis=-1, keepdims=True)
    scores_tan = (
        jnp.einsum("pqhd,khd->phqk", query_tan, keys, preferred_element_type=jnp.float32)
        + jnp.einsum("qhd,pkhd->phqk", query, keys_tan, preferred_element_type=jnp.float32)
    ) * scale
    scores_tan = jnp.where(valid, scores_tan, 0.0)
    weights_tan = weights * (scores_tan - jnp.sum(weights * scores_tan, axis=-1, keepdims=True))
    weights_low = weights.astype(jnp.bfloat16)
    weights_tan_low = weights_tan.astype(jnp.bfloat16)
    output = jnp.einsum("hqk,khd->qhd", weights_low, values, preferred_element_type=jnp.float32)
    output_tan = jnp.einsum(
        "phqk,khd->pqhd", weights_tan_low, values, preferred_element_type=jnp.float32
    ) + jnp.einsum("hqk,pkhd->pqhd", weights_low, values_tan, preferred_element_type=jnp.float32)
    return (output.astype(jnp.bfloat16), output_tan.astype(jnp.bfloat16))


def shards(tokens, probes, norm_gain, w_query, w_key, w_value, query_gain, key_gain, w_out):
    probe_count = probes.shape[0]
    seq_rows = tokens.shape[0]
    width = tokens.shape[1]
    section = w_query.shape[1]
    head_count = section // HEAD_DIM
    value = tokens.astype(jnp.float32)
    tangent = probes.astype(jnp.float32)
    normed, normed_tan = norm_pair(value, tangent, norm_gain)
    rows_all = (
        jnp.concatenate([normed[None], normed_tan], 0)
        .astype(jnp.bfloat16)
        .reshape((probe_count + 1) * seq_rows, width)
    )

    def add_rows(piece):
        return jnp.dot(rows_all, piece, preferred_element_type=jnp.float32)

    def norm_heads(flat, gain):
        full = flat.reshape(probe_count + 1, seq_rows, head_count, HEAD_DIM)
        normal, normal_tan = norm_pair(full[0], full[1:], gain.reshape(head_count, HEAD_DIM))
        return (normal.astype(jnp.bfloat16), normal_tan.astype(jnp.bfloat16))

    pieces = (
        lax.all_gather(w_query, "tm", axis=0, tiled=True),
        lax.all_gather(w_key, "tm", axis=0, tiled=True),
        lax.all_gather(w_value, "tm", axis=0, tiled=True),
    )
    query_flat = add_rows(pieces[0])
    key_flat = add_rows(pieces[1])
    value_flat = add_rows(pieces[2])
    keys, keys_tan = norm_heads(key_flat, key_gain)
    value_low = value_flat.astype(jnp.bfloat16).reshape(probe_count + 1, seq_rows, section)
    pieces = [keys.reshape(seq_rows, section)]
    pieces = pieces + [keys_tan[index].reshape(seq_rows, section) for index in range(probe_count)]
    pieces = pieces + [value_low[index] for index in range(probe_count + 1)]
    packed = jnp.concatenate(pieces, 1)
    margin = extended(packed, (("tm", 0),), WIN)
    query, query_tan = norm_heads(query_flat, query_gain)
    span = margin.shape[0]
    stacked = margin.reshape(span, 2 * (probe_count + 1), head_count, HEAD_DIM)
    keys = stacked[:, 0]
    keys_tan = jnp.moveaxis(stacked[:, 1 : probe_count + 1], 1, 0)
    values = stacked[:, probe_count + 1]
    values_tan = jnp.moveaxis(stacked[:, probe_count + 2 :], 1, 0)
    start_row = lax.axis_index("tm") * seq_rows
    query_place = start_row + jnp.arange(seq_rows, dtype=jnp.int32)
    key_place = start_row - WIN + jnp.arange(span, dtype=jnp.int32)
    valid = window_mask(query_place, key_place, seq_rows * lax.axis_size("tm"))
    output, output_tan = attend(query, query_tan, keys, keys_tan, values, values_tan, valid)
    out_rows = jnp.concatenate(
        [output.reshape(1, seq_rows, section), output_tan.reshape(probe_count, seq_rows, section)],
        0,
    ).reshape((probe_count + 1) * seq_rows, section)
    terms = lax.dot_general(
        out_rows,
        lax.all_gather(w_out, "tm", axis=0, tiled=True),
        (((1,), (1,)), ((), ())),
        preferred_element_type=jnp.float32,
    )
    sums = lax.psum_scatter(
        terms.astype(jnp.bfloat16), "segment", scatter_dimension=1, tiled=True
    ).astype(jnp.float32)
    part_width = sums.shape[1]
    tangent_part = lax.dynamic_slice_in_dim(
        tangent, lax.axis_index("segment") * part_width, part_width, 2
    )
    total_share = lax.psum(
        jnp.sum(
            tangent_part * sums[seq_rows:].reshape(probe_count, seq_rows, part_width), axis=(0, 2)
        ),
        "segment",
    )
    velocity = sums[:seq_rows].astype(jnp.bfloat16)
    density = total_share / (probe_count * math.sqrt(width))
    return (velocity, density)


def solution(mesh):
    placed = (
        P("tm", None),
        P(None, "tm", None),
        P(),
        P("tm", "segment"),
        P("tm", "segment"),
        P("tm", "segment"),
        P("segment"),
        P("segment"),
        P("tm", "segment"),
    )
    return jax.shard_map(
        shards, mesh=mesh, in_specs=placed, out_specs=(P("tm", "segment"), P("tm")), check_vma=False
    )
```

profile of v0, /device:TPU:1, one launch (start us, length us, event | category | flops | bytes accessed | tf_op | source)
XLA Modules:
  0.0 429.8 jit_solution(15059644603630544945)
XLA Ops:
  10.1 1.8 convert_element_type.47
  11.8 1.8 multiply_reduce_fusion.4
  15.6 3.5 multiply_convert_fusion.2
  19.1 2.2 pad_maximum_fusion.1
  21.3 70.5 %all-gather.5.cloned.1.call-done = bf16[2560,1280]{1,0:T(8,128)(2,1)} async-done(((bf16[40,1280]{1,0:T(8,128)(2,1)}), bf16[2560,1280]{1,0:T(8,128)(2,1)}) %all-gather.5.cloned.1.call-update) | async-done | bytes 6553616 | tf_op jit(solution)/shard_map/all_gather | solution.py:89
  91.8 9.3 %fusion.35 = f32[768,1280]{1,0:T(8,128)S(1)} fusion(bf16[768,2560]{1,0:T(8,128)(2,1)} %bitcast.108, bf16[2560,1280]{1,0:T(8,128)(2,1)} %all-gather.5.cloned.1.call-done), kind=kOutput, calls=%fused_computation.81 | convolution fusion | flops 5033164800 | bytes 14417920 | tf_op jit(solution)/shard_map/dot_general | solution.py:80
  101.2 1.8 copy-done.10
  103.0 1.7 slice.84
  105.3 1.5 copy.46
  106.8 3.4 copy.47
  110.2 3.3 slice.66
  113.5 2.9 multiply_reduce_fusion.3
  116.6 2.4 fusion.28
  118.9 3.0 multiply_convert_fusion.4
  121.9 1.8 fusion.34
  125.5 1.0 constant_dynamic-update-slice_fusion
  126.4 42.8 %all-gather.7.cloned.1.call-done = bf16[2560,1280]{1,0:T(8,128)(2,1)} async-done(((bf16[40,1280]{1,0:T(8,128)(2,1)}), bf16[2560,1280]{1,0:T(8,128)(2,1)}) %all-gather.7.cloned.1.call-update) | async-done | bytes 6553616 | tf_op jit(solution)/shard_map/all_gather | solution.py:90
  169.2 9.0 %convolution_convert_fusion.1 = bf16[768,1280]{1,0:T(8,128)(2,1)S(1)} fusion(bf16[768,2560]{1,0:T(8,128)(2,1)} %bitcast.109, bf16[2560,1280]{1,0:T(8,128)(2,1)} %all-gather.7.cloned.1.call-done), kind=kOutput, calls=%fused_computation.16 | convolution fusion | flops 5034147840 | bytes 12451840 | tf_op jit(solution)/shard_map/dot_general | solution.py:80
  178.4 2.4 fusion.33
  181.6 2.1 collective-permute-start.1
  183.8 3.4 collective-permute-start
  187.2 70.0 %all-gather.9.cloned.1.call-done = bf16[2560,1280]{1,0:T(8,128)(2,1)} async-done(((bf16[40,1280]{1,0:T(8,128)(2,1)}), bf16[2560,1280]{1,0:T(8,128)(2,1)}) %all-gather.9.cloned.1.call-update) | async-done | bytes 6553616 | tf_op jit(solution)/shard_map/all_gather | solution.py:88
  257.2 9.3 %fusion.36 = f32[768,1280]{1,0:T(8,128)S(1)} fusion(bf16[768,2560]{1,0:T(8,128)(2,1)} %bitcast.110, bf16[2560,1280]{1,0:T(8,128)(2,1)} %all-gather.9.cloned.1.call-done), kind=kOutput, calls=%fused_computation.82 | convolution fusion | flops 5033164800 | bytes 14417920 | tf_op jit(solution)/shard_map/dot_general | solution.py:80
  266.5 1.2 slice.93
  267.7 1.7 slice.95
  269.3 1.7 copy.51
  271.0 3.5 copy.56
  274.5 4.5 %slice.78 = f32[2,256,10,128]{1,0,3,2:T(2,128)} reshape(f32[512,1280]{0,1:T(8,128)} %copy.56) | data formatting | bytes 5242880 | tf_op jit(solution)/shard_map/slice | solution.py:84
  279.1 3.3 multiply_reduce_fusion.2
  282.6 3.4 multiply_convert_fusion.3
  286.0 5.8 %pad_maximum_fusion = bf16[512,7680]{1,0:T(8,128)(2,1)} fusion(bf16[128,7680]{1,0:T(8,128)(2,1)} %collective-permute-done.1, bf16[256,7680]{1,0:T(8,128)(2,1)S(1)} %copy-done.6, bf16[128,7680]{1,0:T(8,128)(2,1)} %collective-permute-done), kind=kLoop, calls=%fused_computation.5 | loop fusion | flops 23592960 | bytes 15728640 | tf_op jit(solution)/shard_map/concatenate | solution.py:24
  291.8 10.7 %copy.50 = bf16[512,7680]{0,1:T(8,128)(2,1)} copy(bf16[512,7680]{1,0:T(8,128)(2,1)} %pad_maximum_fusion) | data formatting | bytes 15728640 | tf_op jit(solution)/shard_map/concatenate | solution.py:24
  302.4 3.1 fusion.6
  305.5 2.9 fusion.5
  308.4 5.9 %copy.54 = f32[10,256,512]{1,2,0:T(8,128)} copy(f32[10,256,512]{2,1,0:T(8,128)} %fusion.5) | data formatting | bytes 10485760 | tf_op jit(solution)/shard_map/div | solution.py:48
  314.4 5.5 %fusion.32 = (bf16[512,2,10,128]{0,3,2,1:T(8,128)(2,1)}, bf16[512,2,10,128]{0,3,2,1:T(8,128)(2,1)}) fusion(bf16[512,6,10,128]{0,3,2,1:T(8,128)(2,1)} %bitcast.93), kind=kLoop, calls=%fused_computation.78 | loop fusion | bytes 10485760 | tf_op jit(solution)/shard_map/slice | solution.py:108
  319.9 4.5 %copy.75 = bf16[512,2,10,128]{3,0,1,2:T(8,128)(2,1)} copy(bf16[512,2,10,128]{0,3,2,1:T(8,128)(2,1)} %get-tuple-element.3) | data formatting | bytes 5242880
  324.3 8.2 %fusion.15 = f32[10,512,2,256]{3,1,2,0:T(8,128)} fusion(bf16[2,256,10,128]{1,0,3,2:T(2,128)(2,1)} %multiply_convert_fusion.3, bf16[512,6,10,128]{0,3,2,1:T(8,128)(2,1)} %bitcast.94), kind=kOutput, calls=%fused_computation.35 | convolution fusion | flops 671088640 | bytes 13107200 | tf_op jit(solution)/shard_map/pqhd,khd->phqk/dot_general | solution.py:50
  332.6 8.3 %multiply_reduce_fusion = (f32[2,10,256]{2,0,1:T(2,128)S(1)}, f32[2,10,256,512]{2,3,0,1:T(8,128)}) fusion(f32[10,256,512]{1,2,0:T(8,128)S(1)} %bitcast.91, f32[10,128]{1,0:T(8,128)S(1)} %bitcast.118, f32[256,10,128]{0,2,1:T(8,128)S(1)} %bitcast.101, f32[256,10]{0,1:T(8,128)S(1)} %get-tuple-element.12, bf16[512,2,10,128]{3,0,1,2:T(8,128)(2,1)S(1)} %copy-done.9, ...), kind=kOutput, calls=%fused_computation.4 | convolution fusion | flops 685173760 | bytes 30313472 | tf_op jit(solution)/shard_map/qhd,pkhd->phqk/dot_general | solution.py:51
  340.8 5.7 %fusion.2 = f32[10,128,2,256]{3,1,2,0:T(8,128)S(1)} fusion(f32[2,10,256,512]{2,3,0,1:T(8,128)} %get-tuple-element.19, f32[2,10,256]{2,0,1:T(2,128)S(1)} %get-tuple-element.18, f32[10,256,512]{1,2,0:T(8,128)S(1)} %bitcast.91, bf16[512,6,10,128]{0,3,2,1:T(8,128)(2,1)} %bitcast.95), kind=kOutput, calls=%fused_computation.6 | convolution fusion | flops 678952960 | bytes 19681280 | tf_op jit(solution)/shard_map/phqk,khd->pqhd/dot_general | solution.py:58
  347.6 2.4 convolution_convert_fusion.2
  350.1 2.3 copy.63
  352.4 10.0 %convolution_convert_fusion = bf16[768,2560]{1,0:T(8,128)(2,1)} fusion(bf16[768,1280]{1,0:T(8,128)(2,1)} %bitcast.114, bf16[2560,1280]{1,0:T(8,128)(2,1)} %all-gather.11.cloned.1.call-done), kind=kOutput, calls=%fused_computation.12 | convolution fusion | flops 5035130880 | bytes 12451840 | tf_op jit(solution)/shard_map/dot_general | solution.py:118
  362.4 5.2 %convert_element_type.48 = f32[2,256,2560]{2,1,0:T(8,128)} convert(s32[2,256,2560]{2,1,0:T(8,128)} %param.10) | non-fusion elementwise | flops 1310720 | bytes 10485760 | tf_op jit(solution)/shard_map/convert_element_type | solution.py:71
  367.6 46.6 %reduce-scatter.2.cloned.1.call-done = bf16[768,1280]{1,0:T(8,128)(2,1)} async-done(((bf16[768,2560]{1,0:T(8,128)(2,1)}), bf16[768,1280]{1,0:T(8,128)(2,1)}) %reduce-scatter.2.cloned.1.call-update) | async-done | bytes 1966096 | tf_op jit(solution)/shard_map/reduce_scatter | solution.py:124
  414.2 1.3 slice-done.4
  415.5 2.1 fusion.8
  417.6 3.8 psum.7
  (88 shorter events, 11.0 us)
Async XLA Ops:
  7.2 84.6 %all-gather.5.cloned.1.call-start = ((), (), s32[]{:S(2)}) async-start(), calls=%async_computation.1 | async-start | bytes 6656000 | tf_op jit(solution)/shard_map/all_gather | solution.py:89
  7.9 161.3 %all-gather.7.cloned.1.call-start = ((), (), s32[]{:S(2)}) async-start(), calls=%async_computation.2 | async-start | bytes 6656000 | tf_op jit(solution)/shard_map/all_gather | solution.py:90
  8.6 248.6 %all-gather.9.cloned.1.call-start = ((), (), s32[]{:S(2)}) async-start(), calls=%async_computation.3 | async-start | bytes 6656000 | tf_op jit(solution)/shard_map/all_gather | solution.py:88
  9.4 343.0 %all-gather.11.cloned.1.call-start = ((), (), s32[]{:S(2)}) async-start(), calls=%async_computation.4 | async-start | bytes 6656000 | tf_op jit(solution)/shard_map/all_gather | solution.py:120
  10.0 404.3 %reduce-scatter.2.cloned.1.call-start = ((), (), s32[]{:S(2)}) async-start(), calls=%async_computation.5 | async-start | bytes 5898240 | tf_op jit(solution)/shard_map/reduce_scatter | solution.py:124
  10.1 3.6 copy-start
  13.7 1.3 copy-start.7
  13.7 1.3 copy-start.13
  101.1 1.9 copy-start.10
  105.1 1.7 copy-start.2
  113.5 3.0 copy-start.3
  113.5 3.1 copy-start.11
  113.5 3.1 copy-start.14
  169.2 9.0 %copy-start.4 = (bf16[256,7680]{1,0:T(8,128)(2,1)S(1)}, bf16[256,7680]{1,0:T(8,128)(2,1)}, u32[]{:S(2)}) copy-start(bf16[256,7680]{1,0:T(8,128)(2,1)} %constant_dynamic-update-slice_fusion) | copy-start | bytes 11796484
  178.4 3.2 copy-start.5
  181.6 104.3 %collective-permute-start.1 = (bf16[128,7680]{1,0:T(8,128)(2,1)}, bf16[128,7680]{1,0:T(8,128)(2,1)}, u32[]{:S(2)}, u32[]{:S(2)}) collective-permute-start(bf16[128,7680]{1,0:T(8,128)(2,1)} %get-tuple-element.5), channel_id=1, source_target_pairs={{2,0},{4,2},{6,4},{8,6},{10,8},{12,10},{14,12},{16,14},{18,16},{20... | collective-permute-start | bytes 5898248 | tf_op jit(solution)/shard_map/ppermute | solution.py:23
  183.8 102.2 %collective-permute-start = (bf16[128,7680]{1,0:T(8,128)(2,1)}, bf16[128,7680]{1,0:T(8,128)(2,1)}, u32[]{:S(2)}, u32[]{:S(2)}) collective-permute-start(bf16[128,7680]{1,0:T(8,128)(2,1)} %get-tuple-element.4), channel_id=1, source_target_pairs={{0,2},{2,4},{4,6},{6,8},{8,10},{10,12},{12,14},{14,16},{16,18},{18... | collective-permute-start | bytes 5898248 | tf_op jit(solution)/shard_map/ppermute | solution.py:20
  279.1 3.5 copy-start.1
  279.1 3.5 copy-start.15
  282.6 3.4 copy-start.6
  319.9 12.7 %slice-start.2 = ((s8[5242880]{0:T(1024)(128)(4,1)}), s8[1048576]{0:T(1024)(128)(4,1)S(1)}, s32[]{:S(2)}) async-start(s8[5242880]{0:T(1024)(128)(4,1)} %bitcast.90), calls=%async_computation.8 | async-start | bytes 2097152
  324.3 8.2 %slice-start.3 = ((s8[5242880]{0:T(1024)(128)(4,1)}), s8[4194304]{0:T(1024)(128)(4,1)S(1)}, s32[]{:S(2)}) async-start(s8[5242880]{0:T(1024)(128)(4,1)} %bitcast.90), calls=%async_computation.9 | async-start | bytes 8388608
  324.3 8.2 %copy-start.9 = (bf16[512,2,10,128]{3,0,1,2:T(8,128)(2,1)S(1)}, bf16[512,2,10,128]{3,0,1,2:T(8,128)(2,1)}, u32[]{:S(2)}) copy-start(bf16[512,2,10,128]{3,0,1,2:T(8,128)(2,1)} %copy.75) | copy-start | bytes 7864324
  324.3 22.2 %slice-start = ((s8[5242880]{0:T(1024)(128)(4,1)}), s8[4194304]{0:T(1024)(128)(4,1)S(1)}, s32[]{:S(2)}) async-start(s8[5242880]{0:T(1024)(128)(4,1)} %bitcast.88), calls=%async_computation.6 | async-start | bytes 8388608
  332.5 14.0 %slice-start.1 = ((s8[5242880]{0:T(1024)(128)(4,1)}), s8[1048576]{0:T(1024)(128)(4,1)S(1)}, s32[]{:S(2)}) async-start(s8[5242880]{0:T(1024)(128)(4,1)} %bitcast.88), calls=%async_computation.7 | async-start | bytes 2097152
  340.8 5.7 %copy-start.8 = (bf16[512,2,10,128]{0,3,2,1:T(8,128)(2,1)S(1)}, bf16[512,2,10,128]{0,3,2,1:T(8,128)(2,1)}, u32[]{:S(2)}) copy-start(bf16[512,2,10,128]{0,3,2,1:T(8,128)(2,1)} %get-tuple-element.2) | copy-start | bytes 7864324
  414.2 1.3 slice-start.4
  414.2 7.8 %copy-start.12 = (bf16[768,1280]{1,0:T(8,128)(2,1)S(1)}, bf16[768,1280]{1,0:T(8,128)(2,1)}, u32[]{:S(2)}) copy-start(bf16[768,1280]{1,0:T(8,128)(2,1)} %reduce-scatter.2.cloned.1.call-done) | copy-start | bytes 5898244
Sparse Core Ops, SparseCore 0:
  11.3 80.4 all-gather.4
  95.0 74.1 all-gather.6
  172.5 84.6 all-gather.8
  260.3 74.1 all-gather.10
  362.6 51.6 reduce-scatter.1
where the time goes:
time: 437 us; the launch traced here: 430 us
  waiting for transfers between devices  233 us (53%)
  matrix products  66.1 us (15%)
  local copies, waits for them, and re-layouts  64.1 us (15%)
  other arithmetic  42.9 us (10%)
  between operations  14.8 us (3%)
  starting transfers between devices  5.74 us (1%)
    all_gather x1, waiting for transfers between devices, shards(): lax.all_gather(w_key, 'tm', axis=0, tiled=True)  70.5 us
    all_gather x1, waiting for transfers between devices, shards(): lax.all_gather(w_query, 'tm', axis=0, tiled=True)  70 us
    reduce_scatter x1, waiting for transfers between devices, shards(): lax.psum_scatter(terms.astype(jnp.bfloat16), 'segment', scatter_dimension...  46.6 us
    all_gather x1, waiting for transfers between devices, shards(): lax.all_gather(w_value, 'tm', axis=0, tiled=True)  42.8 us
    dot_general x3, matrix products, add_rows(): return jnp.dot(rows_all, piece, preferred_element_type=jnp.float32)  27.6 us
    slice x6, local copies, waits for them, and re-layouts, norm_heads(): full[1:]  17.9 us
    concatenate x1, local copies, waits for them, and re-layouts, extended(): block = jnp.concatenate([low, block, high], axis=dim)  10.7 us
    dot_general x1, matrix products, shards(): lax.dot_general(out_rows, lax.all_gather(w_out, 'tm', axis=0, tiled=True)...  10 us
  transfers between devices with their start and end apart: 7, of which 4 were waited for; matrix products, arithmetic and copies ran while one was open for 36% of the time, Pallas kernels for 0%

commit v1 on v0

--- a/solution.py
+++ b/solution.py
@@ -3,6 +3,8 @@
 import jax
 import jax.numpy as jnp
 from jax import lax
+from jax.experimental import pallas as pl
+from jax.experimental.pallas import tpu as pltpu
 from jax.sharding import PartitionSpec as P
 
 HEAD_DIM = 128
@@ -10,6 +12,158 @@
 
 
 eps = 1e-06
+MESH = pl.DeviceIdType.MESH
+R = 80
+
+def gather_kernel(wk, wv, wq, wo, W, own, stage, got, local_sem, stage_sem, send_sem, recv_sem):
+    me = lax.axis_index("tm")
+    core = lax.rem(me, 2)
+    x = lax.rem(me // 2, 4)
+    yh = lax.rem(me // 8, 2)
+    z = me // 16
+    flip = core == 0
+    a = jnp.where(flip, x, z); b = jnp.where(flip, z, x)
+    sa = jnp.where(flip, 2, 16); sb = jnp.where(flip, 16, 2)
+    ra = jnp.where(flip, 1, 8); rb = jnp.where(flip, 8, 1)
+    def ring(p, d): return lax.rem(p + d + 4, 4)
+    dev_a = [me + (ring(a, 1) - a) * sa, me + (ring(a, -1) - a) * sa]
+    dev_b = [me + (ring(b, 1) - b) * sb, me + (ring(b, -1) - b) * sb]
+    sib = me + 1 - 2 * core
+    dev_y = me + (1 - 2 * yh) * 8
+    barrier = pltpu.get_barrier_semaphore()
+    peers = [sib, dev_y, *dev_a, *dev_b]
+    for d in peers:
+        pl.semaphore_signal(barrier, inc=1, device_id={"tm": d}, device_id_type=MESH)
+    f = jnp.float32
+    mine0 = jnp.where(flip, wk[...].astype(f), wv[...].astype(f))
+    mine1 = jnp.where(flip, wq[...].astype(f), wo[...].astype(f))
+    theirs0 = jnp.where(flip, wv[...].astype(f), wk[...].astype(f))
+    theirs1 = jnp.where(flip, wo[...].astype(f), wq[...].astype(f))
+    stage[...] = jnp.concatenate([theirs0, theirs1], 0).astype(jnp.bfloat16)
+    pl.semaphore_wait(barrier, len(peers))
+    ex = pltpu.make_async_remote_copy(src_ref=stage, dst_ref=got, send_sem=stage_sem.at[0], recv_sem=stage_sem.at[1],
+                                      device_id={"tm": sib}, device_id_type=MESH)
+    ex.start()
+
+    def place(s, aa, y, bb):
+        m = 2 * s + core
+        blk = aa * ra + y * 4 + bb * rb
+        return m, blk
+    def ref_of(m, blk):
+        return W.at[m, pl.ds(pl.multiple_of(blk * R, 16), R)]
+    def send(s, piece, device, slot):
+        m, blk = place(s, *piece)
+        pltpu.make_async_remote_copy(src_ref=ref_of(m, blk), dst_ref=ref_of(m, blk), send_sem=send_sem.at[s, slot],
+            recv_sem=recv_sem.at[m, blk], device_id={"tm": device}, device_id_type=MESH).start()
+    def wait_blk(m, blk):
+        pltpu.make_async_copy(ref_of(m, blk), ref_of(m, blk), recv_sem.at[m, blk]).wait()
+    def arrive(s, piece):
+        wait_blk(*place(s, *piece))
+    def drain(s, slot, rows):
+        pltpu.make_async_copy(W.at[0, pl.ds(0, rows)], W.at[0, pl.ds(0, rows)], send_sem.at[s, slot]).wait()
+
+    def spread_a(s, piece):
+        send(s, piece, dev_a[0], 0); send(s, piece, dev_a[1], 1)
+    def spread_b(s, piece):
+        send(s, piece, dev_b[0], 2); send(s, piece, dev_b[1], 3)
+    def to_sib(s, piece):
+        send(s, piece, sib, 4)
+    ex.wait()
+    g = got[...].astype(f)
+    for s, mine in ((0, mine0), (1, mine1)):
+        other = g[40 * s:40 * s + 40]
+        both = jnp.where(flip, jnp.concatenate([mine, other], 0), jnp.concatenate([other, mine], 0))
+        own[s] = both.astype(jnp.bfloat16)
+    cps = []
+    for s in range(2):
+        m, blk = place(s, a, yh, b)
+        c = pltpu.make_async_copy(own.at[s], ref_of(m, blk), local_sem.at[s]); c.start(); cps.append(c)
+    for c in cps: c.wait()
+    for s in range(2):
+        send(s, (a, yh, b), dev_y, 5)
+        spread_a(s, (a, yh, b))
+    for s in range(2):
+        if s == 0:
+            spread_b(0, (a, yh, b))
+        to_sib(s, (a, yh, b))
+    def stage_a(s, with_b):
+        arrive(s, (a, 1 - yh, b))
+        spread_a(s, (a, 1 - yh, b))
+        if with_b: spread_b(s, (a, 1 - yh, b))
+        to_sib(s, (a, 1 - yh, b))
+        def body(i, _):
+            y = jnp.where(i == 0, yh, 1 - yh)
+            d = 1 - 2 * y
+            first = ring(a, -d)
+            last = ring(a, d)
+            arrive(s, (first, y, b))
+            fwd = me + (ring(a, d) - a) * sa
+            send(s, (first, y, b), fwd, y)
+            if with_b: spread_b(s, (first, y, b))
+            to_sib(s, (first, y, b))
+            arrive(s, (last, y, b))
+            if with_b: spread_b(s, (last, y, b))
+            to_sib(s, (last, y, b))
+            return 0
+        lax.fori_loop(0, 2, body, 0)
+        def body2(y, _):
+            arrive(s, (ring(a, 2), y, b))
+            if with_b: spread_b(s, (ring(a, 2), y, b))
+            to_sib(s, (ring(a, 2), y, b))
+            return 0
+        lax.fori_loop(0, 2, body2, 0)
+    order = lambda i: (jnp.where(i // 2 == 0, a, jnp.where(i // 2 == 1, ring(a, 1), jnp.where(i // 2 == 2, ring(a, -1), ring(a, 2)))), jnp.where(lax.rem(i, 2) == 0, yh, 1 - yh))
+    def late_b(s):
+        def body(i, _):
+            aa, y = order(i)
+            spread_b(s, (aa, y, b))
+            return 0
+        lax.fori_loop(0, 8, body, 0)
+    def stage_b(s):
+        def body(i, _):
+            aa, y = order(i)
+            d = 1 - 2 * y
+            p1 = (aa, y, ring(b, -d)); p2 = (aa, y, ring(b, d))
+            arrive(s, p1)
+            send(s, p1, me + (ring(b, d) - b) * sb, 2 + y)
+            to_sib(s, p1)
+            arrive(s, p2)
+            to_sib(s, p2)
+            return 0
+        lax.fori_loop(0, 8, body, 0)
+    def stage_c(s):
+        def body(i, _):
+            aa, y = order(i)
+            p = (aa, y, ring(b, 2))
+            arrive(s, p); to_sib(s, p)
+            return 0
+        lax.fori_loop(0, 8, body, 0)
+    stage_a(0, True)
+    stage_a(1, False)
+    stage_b(0)
+    late_b(1)
+    stage_c(0)
+    stage_b(1)
+    stage_c(1)
+    def fin(i, _):
+        wait_blk(2 * (i // 32) + 1 - core, lax.rem(i, 32))
+        return 0
+    lax.fori_loop(0, 64, fin, 0)
+    for s in range(2):
+        for slot, n in ((0, 3), (1, 3), (2, 12), (3, 12), (4, 32), (5, 1)):
+            drain(s, slot, n * R)
+
+def gather(wk, wv, wq, wo, vmem):
+    sp = pl.BlockSpec(memory_space=pltpu.VMEM)
+    return pl.pallas_call(
+        gather_kernel,
+        out_shape=jax.ShapeDtypeStruct((4, 2560, 1280), jnp.bfloat16),
+        in_specs=[sp] * 4,
+        out_specs=pl.BlockSpec(memory_space=pltpu.VMEM if vmem else pl.ANY),
+        scratch_shapes=[pltpu.VMEM((2, R, 1280), jnp.bfloat16), pltpu.VMEM((R, 1280), jnp.bfloat16), pltpu.VMEM((R, 1280), jnp.bfloat16),
+            pltpu.SemaphoreType.DMA((2,)), pltpu.SemaphoreType.DMA((2,)), pltpu.SemaphoreType.DMA((2, 6)), pltpu.SemaphoreType.DMA((4, 32))],
+        compiler_params=pltpu.CompilerParams(collective_id=0, has_side_effects=True, vmem_limit_bytes=60 * 2**20),
+    )(wk, wv, wq, wo)
 
 
 def extended(block, sides, width):
@@ -84,11 +238,8 @@
         normal, normal_tan = norm_pair(full[0], full[1:], gain.reshape(head_count, HEAD_DIM))
         return (normal.astype(jnp.bfloat16), normal_tan.astype(jnp.bfloat16))
 
-    pieces = (
-        lax.all_gather(w_query, "tm", axis=0, tiled=True),
-        lax.all_gather(w_key, "tm", axis=0, tiled=True),
-        lax.all_gather(w_value, "tm", axis=0, tiled=True),
-    )
+    whole = gather(w_key, w_value, w_query, w_out, False)
+    pieces = (whole[2], whole[0], whole[1])
     query_flat = add_rows(pieces[0])
     key_flat = add_rows(pieces[1])
     value_flat = add_rows(pieces[2])
@@ -116,26 +267,19 @@
         0,
     ).reshape((probe_count + 1) * seq_rows, section)
     terms = lax.dot_general(
-        out_rows,
-        lax.all_gather(w_out, "tm", axis=0, tiled=True),
-        (((1,), (1,)), ((), ())),
-        preferred_element_type=jnp.float32,
-    )
-    sums = lax.psum_scatter(
-        terms.astype(jnp.bfloat16), "segment", scatter_dimension=1, tiled=True
-    ).astype(jnp.float32)
-    part_width = sums.shape[1]
-    tangent_part = lax.dynamic_slice_in_dim(
-        tangent, lax.axis_index("segment") * part_width, part_width, 2
-    )
-    total_share = lax.psum(
-        jnp.sum(
-            tangent_part * sums[seq_rows:].reshape(probe_count, seq_rows, part_width), axis=(0, 2)
-        ),
-        "segment",
-    )
-    velocity = sums[:seq_rows].astype(jnp.bfloat16)
-    density = total_share / (probe_count * math.sqrt(width))
+        out_rows, whole[3], (((1,), (1,)), ((), ())), preferred_element_type=jnp.float32
+    )
+    part_width = width // 2
+    side = lax.axis_index("segment")
+    away = lax.dynamic_slice_in_dim(terms[:seq_rows], (1 - side) * part_width, part_width, 1)
+    near = lax.dynamic_slice_in_dim(terms[:seq_rows], side * part_width, part_width, 1)
+    share = lax.ppermute(away.astype(jnp.bfloat16), "segment", [(0, 1), (1, 0)])
+    velocity = (near + share.astype(jnp.float32)).astype(jnp.bfloat16)
+    total = jnp.sum(
+        tangent * terms[seq_rows:].reshape(probe_count, seq_rows, width), axis=(0, 2)
+    )
+    total = total + lax.ppermute(total, "segment", [(0, 1), (1, 0)])
+    density = total / (probe_count * math.sqrt(width))
     return (velocity, density)
 
 

time: 437 us -> 280 us (0.64)
  waiting for transfers between devices: 233 us -> 13.4 us
  Pallas kernels: 0 us -> 89 us
  between operations: 14.8 us -> 1.48 us
  other arithmetic: 42.9 us -> 34.5 us
    all_gather x4 -> x0, waiting for transfers between devices: 183 us -> none  [the longest x1 70.5 us: shards(): lax.all_gather(w_key, 'tm', axis=0, tiled=True)]
    pallas_call x0 -> x1, Pallas kernels: none -> 89 us  [gather(): pl.pallas_call(gather_kernel, out_shape=jax.ShapeDtypeStruct((4, 2560, 12...]
    reduce_scatter x1 -> x0, waiting for transfers between devices: 46.6 us -> none  [shards(): lax.psum_scatter(terms.astype(jnp.bfloat16), 'segment', scatter_dimension...]
    ppermute x0 -> x2, waiting for transfers between devices: none -> 13.4 us  [the longest x1 13.4 us: shards(): total = total + lax.ppermute(total, 'segment', [(0, 1), (1, 0)])]
    unnamed x47 -> x53, local copies, waits for them, and re-layouts: 9.51 us -> 13.6 us
  transfers between devices with their start and end apart: 7 -> 4, of which waited for: 4 -> 1; matrix products, arithmetic and copies ran while one was open for 36% -> 11% of each run, Pallas kernels for 0% -> 0%
where the time goes in v1:
time: 280 us; the launch traced here: 275 us
  Pallas kernels  89 us (32%)
  local copies, waits for them, and re-layouts  66.2 us (24%)
  matrix products  64 us (23%)
  other arithmetic  34.5 us (12%)
  waiting for transfers between devices  13.4 us (5%)
  starting transfers between devices  6.5 us (2%)
    pallas_call x1, Pallas kernels, gather(): pl.pallas_call(gather_kernel, out_shape=jax.ShapeDtypeStruct((4, 2560, 12...  89 us
    dot_general x3, matrix products, add_rows(): return jnp.dot(rows_all, piece, preferred_element_type=jnp.float32)  26.6 us
    slice x6, local copies, waits for them, and re-layouts, norm_heads(): full[1:]  17.6 us
    unnamed x53, local copies, waits for them, and re-layouts  13.6 us
    ppermute x1, waiting for transfers between devices, shards(): total = total + lax.ppermute(total, 'segment', [(0, 1), (1, 0)])  13.4 us
    concatenate x1, local copies, waits for them, and re-layouts, extended(): block = jnp.concatenate([low, block, high], axis=dim)  10.6 us
    dot_general x1, matrix products, attend(): jnp.einsum('qhd,pkhd->phqk', query, keys_tan, preferred_element_type=jnp....  8.12 us
    dot_general x1, matrix products, shards(): lax.dot_general(out_rows, whole[3], (((1,), (1,)), ((), ())), preferred_e...  8.04 us
  transfers between devices with their start and end apart: 4, of which 1 were waited for; matrix products, arithmetic and copies ran while one was open for 11% of the time, Pallas kernels for 0%

profile of v1, /device:TPU:1, one launch (start us, length us, event | category | flops | bytes accessed | tf_op | source)
XLA Modules:
  0.0 275.2 jit_solution(6293345340524855411)
XLA Ops:
  0.6 1.8 convert_element_type.65
  2.4 1.8 multiply_reduce_fusion.5
  6.2 1.0 multiply_convert_fusion.2
  7.5 89.0 %shard_map.104 = bf16[4,2560,1280]{2,1,0:T(8,128)(2,1)} custom-call(bf16[40,1280]{1,0:T(8,128)(2,1)} %wk.1, bf16[40,1280]{1,0:T(8,128)(2,1)} %wv.1, bf16[40,1280]{1,0:T(8,128)(2,1)} %wq.1, bf16[40,1280]{1,0:T(8,128)(2,1)} %wo.1), custom_call_target="tpu_custom_call" | custom-call | tf_op jit(solution)/shard_map/pallas_call | solution.py:158
  96.6 8.1 %fusion.8 = f32[768,1280]{1,0:T(8,128)S(1)} fusion(bf16[768,2560]{1,0:T(8,128)(2,1)S(1)} %bitcast.119, bf16[4,2560,1280]{2,1,0:T(8,128)(2,1)} %shard_map.104), kind=kOutput, calls=%fused_computation.12 | convolution fusion | flops 5033164800 | bytes 14417920 | tf_op jit(solution)/shard_map/dot_general | solution.py:234
  104.8 1.6 slice.99
  106.4 1.5 copy-done.9
  107.9 1.2 copy-done.12
  109.2 9.2 %fusion.19 = bf16[768,1280]{1,0:T(8,128)(2,1)} fusion(bf16[768,2560]{1,0:T(8,128)(2,1)S(1)} %bitcast.121, bf16[4,2560,1280]{2,1,0:T(8,128)(2,1)} %shard_map.104), kind=kOutput, calls=%fused_computation.28 | convolution fusion | flops 5034147840 | bytes 12451840 | tf_op jit(solution)/shard_map/dot_general | solution.py:234
  119.0 1.5 copy.46
  120.5 3.2 %copy.47 = f32[512,1280]{0,1:T(8,128)} copy(f32[512,1280]{1,0:T(8,128)} %slice.99) | data formatting | bytes 5242880 | tf_op jit(solution)/shard_map/slice | solution.py:238
  123.7 3.3 %slice.78 = f32[2,256,10,128]{1,0,3,2:T(2,128)S(1)} reshape(f32[512,1280]{0,1:T(8,128)} %copy.47) | data formatting | bytes 5242880 | tf_op jit(solution)/shard_map/slice | solution.py:238
  127.0 2.9 %multiply_reduce_fusion.4 = f32[2,256,10]{1,0,2:T(2,128)S(1)} fusion(f32[2,256,10,128]{1,0,3,2:T(2,128)S(1)} %slice.78, f32[256,10,128]{0,2,1:T(8,128)} %bitcast.115), kind=kLoop, calls=%fused_computation.38 | loop fusion | flops 1305600 | bytes 3952640 | tf_op jit(solution)/shard_map/reduce_sum | solution.py:185
  130.1 2.3 fusion.42
  132.4 3.5 %multiply_convert_fusion.4 = bf16[2,256,10,128]{1,0,3,2:T(2,128)(2,1)S(1)} fusion(f32[2,256,10,128]{1,0,3,2:T(2,128)S(1)} %slice.78, f32[10,128]{1,0:T(8,128)S(1)} %bitcast.126, f32[2,256,10]{1,0,2:T(2,128)S(1)} %broadcast_multiply_fusion.3, f32[256,10,128]{0,2,1:T(8,128)S(1)} %broadcast_multiply_fusion.1, f32[256,10]{0,1:T(8,128)S(1)} %get-tuple-element.11), kind=kLoop, calls=%fused_computation.37 | loop fusion | flops 3276800 | bytes 5278720 | tf_op jit(solution)/shard_map/convert_element_type | solution.py:239
  136.0 1.8 fusion.48
  138.6 0.9 constant_dynamic-update-slice_fusion.1
  139.5 0.9 constant_dynamic-update-slice_fusion
  140.5 0.9 slice_dynamic-update-slice_fusion.2
  141.4 1.0 slice_dynamic-update-slice_fusion.1
  142.4 0.9 slice_dynamic-update-slice_fusion
  143.3 4.3 %fusion.47 = (bf16[128,7680]{1,0:T(8,128)(2,1)}, bf16[128,7680]{1,0:T(8,128)(2,1)}) fusion(bf16[256,7680]{1,0:T(8,128)(2,1)} %slice_dynamic-update-slice_fusion), kind=kLoop, calls=%fused_computation.91 | loop fusion | bytes 7864320 | tf_op jit(solution)/shard_map/slice | solution.py:175
  147.6 2.0 collective-permute-start.1
  149.6 3.5 %collective-permute-start = (bf16[128,7680]{1,0:T(8,128)(2,1)}, bf16[128,7680]{1,0:T(8,128)(2,1)}, u32[]{:S(2)}, u32[]{:S(2)}) collective-permute-start(bf16[128,7680]{1,0:T(8,128)(2,1)} %get-tuple-element.4), channel_id=1, source_target_pairs={{0,2},{2,4},{4,6},{6,8},{8,10},{10,12},{12,14},{14,16},{16,18},{18... | collective-permute-start | bytes 5898248 | tf_op jit(solution)/shard_map/ppermute | solution.py:174
  153.2 9.3 %fusion.4 = f32[768,1280]{1,0:T(8,128)S(1)} fusion(bf16[768,2560]{1,0:T(8,128)(2,1)} %bitcast.120, bf16[4,2560,1280]{2,1,0:T(8,128)(2,1)} %shard_map.104), kind=kOutput, calls=%fused_computation.8 | convolution fusion | flops 5033164800 | bytes 14417920 | tf_op jit(solution)/shard_map/dot_general | solution.py:234
  162.5 1.2 slice.108
  163.7 1.6 slice.110
  165.3 1.7 copy.51
  167.1 3.4 %copy.56 = f32[512,1280]{0,1:T(8,128)} copy(f32[512,1280]{1,0:T(8,128)} %slice.110) | data formatting | bytes 5242880 | tf_op jit(solution)/shard_map/slice | solution.py:238
  170.5 4.5 %slice.92 = f32[2,256,10,128]{1,0,3,2:T(2,128)} reshape(f32[512,1280]{0,1:T(8,128)} %copy.56) | data formatting | bytes 5242880 | tf_op jit(solution)/shard_map/slice | solution.py:238
  175.6 3.3 %multiply_reduce_fusion.3 = f32[2,256,10]{1,0,2:T(2,128)S(1)} fusion(f32[2,256,10,128]{1,0,3,2:T(2,128)} %slice.92, f32[256,10,128]{0,2,1:T(8,128)S(1)} %bitcast.109), kind=kLoop, calls=%fused_computation.36 | loop fusion | flops 1305600 | bytes 3952640 | tf_op jit(solution)/shard_map/reduce_sum | solution.py:185
  179.1 3.4 %multiply_convert_fusion.3 = bf16[2,256,10,128]{1,0,3,2:T(2,128)(2,1)} fusion(f32[2,256,10,128]{1,0,3,2:T(2,128)S(1)} %copy-done.2, f32[10,128]{1,0:T(8,128)S(1)} %bitcast.127, f32[2,256,10]{1,0,2:T(2,128)S(1)} %broadcast_multiply_fusion.2, f32[256,10,128]{0,2,1:T(8,128)S(1)} %broadcast_multiply_fusion, f32[256,10]{0,1:T(8,128)S(1)} %get-tuple-element.12), kind=kLoop, calls=%fused_computation.35 | loop fusion | flops 3276800 | bytes 5278720 | tf_op jit(solution)/shard_map/convert_element_type | solution.py:239
  182.4 5.8 %pad_maximum_fusion = bf16[512,7680]{1,0:T(8,128)(2,1)} fusion(bf16[128,7680]{1,0:T(8,128)(2,1)} %collective-permute-done.1, bf16[256,7680]{1,0:T(8,128)(2,1)S(1)} %copy-done.5, bf16[128,7680]{1,0:T(8,128)(2,1)} %collective-permute-done), kind=kLoop, calls=%fused_computation.5 | loop fusion | flops 23592960 | bytes 15728640 | tf_op jit(solution)/shard_map/concatenate | solution.py:178
  188.3 10.6 %copy.50 = bf16[512,7680]{0,1:T(8,128)(2,1)} copy(bf16[512,7680]{1,0:T(8,128)(2,1)} %pad_maximum_fusion) | data formatting | bytes 15728640 | tf_op jit(solution)/shard_map/concatenate | solution.py:178
  198.9 3.3 %fusion.18 = (f32[10,256]{1,0:T(8,128)S(1)}, f32[10,256,512]{2,1,0:T(8,128)S(1)}) fusion(pred[256,512]{1,0:T(8,128)(4,1)S(1)} %fusion.45, bf16[512,6,10,128]{0,3,2,1:T(8,128)(2,1)} %bitcast.103, f32[256,10,128]{0,2,1:T(8,128)S(1)} %bitcast.111, f32[10,128]{1,0:T(8,128)S(1)} %bitcast.128, f32[256,10]{0,1:T(8,128)S(1)} %get-tuple-element.12), kind=kOutput, calls=%fused_computation.26 | convolution fusion | flops 340456960 | bytes 8020992 | tf_op jit(solution)/shard_map/qhd,khd->hqk/dot_general | solution.py:200
  202.5 2.6 fusion.46
  205.1 2.8 %fusion.17 = f32[10,256,512]{2,1,0:T(8,128)} fusion(f32[10,256,512]{2,1,0:T(8,128)S(1)} %get-tuple-element.17, f32[10,256]{1,0:T(8,128)S(1)} %get-tuple-element.16, pred[256,512]{1,0:T(8,128)(4,1)S(1)} %fusion.45), kind=kLoop, calls=%fused_computation.25 | loop fusion | flops 3932160 | bytes 10627072 | tf_op jit(solution)/shard_map/div | solution.py:202
  207.9 5.9 %copy.54 = f32[10,256,512]{1,2,0:T(8,128)} copy(f32[10,256,512]{2,1,0:T(8,128)} %fusion.17) | data formatting | bytes 10485760 | tf_op jit(solution)/shard_map/div | solution.py:202
  213.9 3.9 %convolution_convert_fusion = bf16[10,128,256]{2,1,0:T(8,128)(2,1)S(1)} fusion(f32[10,256,512]{2,1,0:T(8,128)} %fusion.17, bf16[512,6,10,128]{0,3,2,1:T(8,128)(2,1)} %bitcast.104), kind=kOutput, calls=%fused_computation.43 | convolution fusion | flops 337182720 | bytes 7208960 | tf_op jit(solution)/shard_map/hqk,khd->qhd/dot_general | solution.py:211
  217.8 4.5 %copy.75 = bf16[512,2,10,128]{3,0,1,2:T(8,128)(2,1)} copy(bf16[512,2,10,128]{0,3,2,1:T(8,128)(2,1)} %get-tuple-element.3) | data formatting | bytes 5242880
  222.3 7.6 %fusion.29 = f32[10,512,2,256]{3,1,2,0:T(8,128)} fusion(bf16[2,256,10,128]{1,0,3,2:T(2,128)(2,1)} %multiply_convert_fusion.3, bf16[512,6,10,128]{0,3,2,1:T(8,128)(2,1)} %bitcast.105), kind=kOutput, calls=%fused_computation.45 | convolution fusion | flops 671088640 | bytes 13107200 | tf_op jit(solution)/shard_map/pqhd,khd->phqk/dot_general | solution.py:204
  229.9 8.1 %multiply_reduce_fusion = (f32[2,10,256]{2,0,1:T(2,128)S(1)}, f32[2,10,256,512]{2,3,0,1:T(8,128)}) fusion(f32[10,256,512]{1,2,0:T(8,128)S(1)} %bitcast.102, f32[10,128]{1,0:T(8,128)S(1)} %bitcast.129, f32[256,10,128]{0,2,1:T(8,128)S(1)} %bitcast.112, f32[256,10]{0,1:T(8,128)S(1)} %get-tuple-element.12, bf16[512,2,10,128]{3,0,1,2:T(8,128)(2,1)S(1)} %copy-done.8, ...), kind=kOutput, calls=%fused_computation.4 | convolution fusion | flops 685173760 | bytes 30313472 | tf_op jit(solution)/shard_map/qhd,pkhd->phqk/dot_general | solution.py:205
  238.0 5.7 %fusion.14 = f32[10,128,2,256]{3,1,2,0:T(8,128)S(1)} fusion(f32[2,10,256,512]{2,3,0,1:T(8,128)} %get-tuple-element.19, f32[2,10,256]{2,0,1:T(2,128)S(1)} %get-tuple-element.18, f32[10,256,512]{1,2,0:T(8,128)S(1)} %bitcast.102, bf16[512,6,10,128]{0,3,2,1:T(8,128)(2,1)} %bitcast.106), kind=kOutput, calls=%fused_computation.18 | convolution fusion | flops 678952960 | bytes 19681280 | tf_op jit(solution)/shard_map/phqk,khd->pqhd/dot_general | solution.py:212
  244.9 2.3 copy.63
  247.2 8.0 %fusion.2 = f32[768,2560]{1,0:T(8,128)S(1)} fusion(bf16[768,1280]{1,0:T(8,128)(2,1)} %bitcast.125, bf16[4,2560,1280]{2,1,0:T(8,128)(2,1)} %shard_map.104), kind=kOutput, calls=%fused_computation.6 | convolution fusion | flops 5033164800 | bytes 16384000 | tf_op jit(solution)/shard_map/dot_general | solution.py:269
  256.4 1.1 slice-done.2
  258.9 13.4 %collective-permute-done.3 = f32[256]{0:T(256)S(1)} collective-permute-done((f32[256]{0:T(256)S(1)}, f32[256]{0:T(256)S(1)}, u32[]{:S(2)}, u32[]{:S(2)}) %collective-permute-start.3) | collective-permute-done | bytes 1056 | tf_op jit(solution)/shard_map/ppermute | solution.py:281
  272.9 2.1 add_convert_fusion
  (84 shorter events, 9.2 us)
Async XLA Ops:
  0.6 3.6 %copy-start = (s32[2,256,2560]{2,1,0:T(8,128)S(1)}, s32[2,256,2560]{2,1,0:T(8,128)}, u32[]{:S(2)}) copy-start(s32[2,256,2560]{2,1,0:T(8,128)} %param.10) | copy-start | bytes 15728644
  4.2 1.3 copy-start.6
  4.2 1.3 copy-start.14
  7.5 89.0 %copy-start.11 = (bf16[3,256,2560]{2,1,0:T(8,128)(2,1)}, bf16[3,256,2560]{2,1,0:T(8,128)(2,1)S(1)}, u32[]{:S(2)}) copy-start(bf16[3,256,2560]{2,1,0:T(8,128)(2,1)S(1)} %pad_maximum_fusion.1) | copy-start | bytes 11796484
  104.7 3.3 %copy-start.9 = (f32[768,1280]{1,0:T(8,128)}, f32[768,1280]{1,0:T(8,128)S(1)}, u32[]{:S(2)}) copy-start(f32[768,1280]{1,0:T(8,128)S(1)} %fusion.8) | copy-start | bytes 11796484
  104.8 4.4 %copy-start.12 = (bf16[3,256,2560]{2,1,0:T(8,128)(2,1)S(1)}, bf16[3,256,2560]{2,1,0:T(8,128)(2,1)}, u32[]{:S(2)}) copy-start(bf16[3,256,2560]{2,1,0:T(8,128)(2,1)} %copy-done.11) | copy-start | bytes 11796484
  118.8 1.8 copy-start.3
  127.0 3.0 %copy-start.4 = (f32[256,1280]{0,1:T(8,128)S(1)}, f32[256,1280]{0,1:T(8,128)}, u32[]{:S(2)}) copy-start(f32[256,1280]{0,1:T(8,128)} %copy-done.3) | copy-start | bytes 3932164
  127.0 3.1 %copy-start.10 = (f32[256,1280]{1,0:T(8,128)S(1)}, f32[256,1280]{1,0:T(8,128)}, u32[]{:S(2)}) copy-start(f32[256,1280]{1,0:T(8,128)} %copy.46) | copy-start | bytes 3932164
  127.0 3.1 %copy-start.15 = (f32[1280]{0:T(1024)S(1)}, f32[1280]{0:T(1024)}, u32[]{:S(2)}) copy-start(f32[1280]{0:T(1024)} %param.16) | copy-start | bytes 15364
  138.6 1.9 copy-start.13
  147.6 34.8 %collective-permute-start.1 = (bf16[128,7680]{1,0:T(8,128)(2,1)}, bf16[128,7680]{1,0:T(8,128)(2,1)}, u32[]{:S(2)}, u32[]{:S(2)}) collective-permute-start(bf16[128,7680]{1,0:T(8,128)(2,1)} %get-tuple-element.5), channel_id=1, source_target_pairs={{2,0},{4,2},{6,4},{8,6},{10,8},{12,10},{14,12},{16,14},{18,16},{20... | collective-permute-start | bytes 5898248 | tf_op jit(solution)/shard_map/ppermute | solution.py:177
  149.6 32.8 %collective-permute-start = (bf16[128,7680]{1,0:T(8,128)(2,1)}, bf16[128,7680]{1,0:T(8,128)(2,1)}, u32[]{:S(2)}, u32[]{:S(2)}) collective-permute-start(bf16[128,7680]{1,0:T(8,128)(2,1)} %get-tuple-element.4), channel_id=1, source_target_pairs={{0,2},{2,4},{4,6},{6,8},{8,10},{10,12},{12,14},{14,16},{16,18},{18... | collective-permute-start | bytes 5898248 | tf_op jit(solution)/shard_map/ppermute | solution.py:174
  175.5 3.5 %copy-start.2 = (f32[2,256,10,128]{1,0,3,2:T(2,128)S(1)}, f32[2,256,10,128]{1,0,3,2:T(2,128)}, u32[]{:S(2)}) copy-start(f32[2,256,10,128]{1,0,3,2:T(2,128)} %slice.92) | copy-start | bytes 7864324
  175.5 3.5 %copy-start.16 = (f32[1280]{0:T(1024)S(1)}, f32[1280]{0:T(1024)}, u32[]{:S(2)}) copy-start(f32[1280]{0:T(1024)} %param.15) | copy-start | bytes 15364
  179.1 3.4 %copy-start.5 = (bf16[256,7680]{1,0:T(8,128)(2,1)S(1)}, bf16[256,7680]{1,0:T(8,128)(2,1)}, u32[]{:S(2)}) copy-start(bf16[256,7680]{1,0:T(8,128)(2,1)} %slice_dynamic-update-slice_fusion) | copy-start | bytes 11796484
  198.9 3.6 %copy-start.1 = (bf16[512,7680]{0,1:T(8,128)(2,1)S(1)}, bf16[512,7680]{0,1:T(8,128)(2,1)}, u32[]{:S(2)}) copy-start(bf16[512,7680]{0,1:T(8,128)(2,1)} %copy.50) | copy-start | bytes 23592964
  217.8 12.1 %slice-start.4 = ((s8[5242880]{0:T(1024)(128)(4,1)}), s8[1048576]{0:T(1024)(128)(4,1)S(1)}, s32[]{:S(2)}) async-start(s8[5242880]{0:T(1024)(128)(4,1)} %bitcast.101), calls=%async_computation.4 | async-start | bytes 2097152
  222.3 7.6 %slice-start.5 = ((s8[5242880]{0:T(1024)(128)(4,1)}), s8[4194304]{0:T(1024)(128)(4,1)S(1)}, s32[]{:S(2)}) async-start(s8[5242880]{0:T(1024)(128)(4,1)} %bitcast.101), calls=%async_computation.5 | async-start | bytes 8388608
  222.3 7.6 %copy-start.8 = (bf16[512,2,10,128]{3,0,1,2:T(8,128)(2,1)S(1)}, bf16[512,2,10,128]{3,0,1,2:T(8,128)(2,1)}, u32[]{:S(2)}) copy-start(bf16[512,2,10,128]{3,0,1,2:T(8,128)(2,1)} %copy.75) | copy-start | bytes 7864324
  222.3 21.4 %slice-start = ((s8[5242880]{0:T(1024)(128)(4,1)}), s8[4194304]{0:T(1024)(128)(4,1)S(1)}, s32[]{:S(2)}) async-start(s8[5242880]{0:T(1024)(128)(4,1)} %bitcast.97), calls=%async_computation | async-start | bytes 8388608
  229.9 13.9 %slice-start.1 = ((s8[5242880]{0:T(1024)(128)(4,1)}), s8[1048576]{0:T(1024)(128)(4,1)S(1)}, s32[]{:S(2)}) async-start(s8[5242880]{0:T(1024)(128)(4,1)} %bitcast.97), calls=%async_computation.1 | async-start | bytes 2097152
  238.0 5.7 %copy-start.7 = (bf16[512,2,10,128]{0,3,2,1:T(8,128)(2,1)S(1)}, bf16[512,2,10,128]{0,3,2,1:T(8,128)(2,1)}, u32[]{:S(2)}) copy-start(bf16[512,2,10,128]{0,3,2,1:T(8,128)(2,1)} %get-tuple-element.2) | copy-start | bytes 7864324
  255.3 2.2 slice-start.2
  255.5 2.3 slice-start.3
  255.9 17.0 %collective-permute-start.2 = (bf16[256,1280]{1,0:T(8,128)(2,1)S(1)}, bf16[256,1280]{1,0:T(8,128)(2,1)}, u32[]{:S(2)}, u32[]{:S(2)}) collective-permute-start(bf16[256,1280]{1,0:T(8,128)(2,1)S(1)} %dynamic-slice_convert_fusion), channel_id=1, source_target_pairs={{0,1},{1,0},{2,3},{3,2},{4,5},{5,4},{6,7},{7,6},{8,9},{9,8},{10,11... | collective-permute-start | bytes 1966088 | tf_op jit(solution)/shard_map/ppermute | solution.py:276
  258.4 13.9 %collective-permute-start.3 = (f32[256]{0:T(256)S(1)}, f32[256]{0:T(256)S(1)}, u32[]{:S(2)}, u32[]{:S(2)}) collective-permute-start(f32[256]{0:T(256)S(1)} %multiply_reduce_fusion.1), channel_id=1, source_target_pairs={{0,1},{1,0},{2,3},{3,2},{4,5},{5,4},{6,7},{7,6},{8,9},{9,8},{10,11... | collective-permute-start | bytes 3080 | tf_op jit(solution)/shard_map/ppermute | solution.py:281

commit v2 on v0

v2 whole, which is shorter than its diff:
```python
import math

import jax
import jax.numpy as jnp
from jax import lax
from jax.experimental import pallas as pl
from jax.experimental.pallas import tpu as pltpu
from jax.sharding import PartitionSpec as P

MESH = pl.DeviceIdType.MESH
HEAD = 128
WIN = 128
EPS = 1e-06
BF = jnp.bfloat16
F32 = jnp.float32

ROWS = 256
WIDTH = 2560
SEC = 1280
HALF = 640
PIECE = 80
HEADS = 10
ROW_BLOCK = 16

UNITS = 3


def norm_pair(value, tangents, gain):
    factor = lax.rsqrt(jnp.mean(value * value, axis=-1, keepdims=True) + EPS)
    cube = factor * factor * factor
    outs = [value * factor * gain]
    for tangent in tangents:
        inner = jnp.mean(value * tangent, axis=-1, keepdims=True)
        outs.append((tangent * factor - value * (cube * inner)) * gain)
    return outs


def kernel(
    tokens_hbm, probes_hbm, gain_ref, wq, wk, wv, wo, qgain, kgain,
    velocity_ref, density_ref,
    W, tokens, probes, h, ext, q, o, near, away, share, dens, dens_in,
    own_kv, own_q, own_o, stage, got,
    in_sem, stage_sem, local_sem, y_sem, send_sem, pair_sem, opp_sem, sib_sem, halo_send, halo_recv, out_sem,
):
    me = lax.axis_index("tm")
    side = lax.axis_index("segment")
    core = lax.rem(me, 2)
    x = lax.rem(me // 2, 4)
    yh = lax.rem(me // 8, 2)
    z = me // 16
    flip = core == 0
    a = jnp.where(flip, x, z)
    b = jnp.where(flip, z, x)
    sa = jnp.where(flip, 2, 16)
    sb = jnp.where(flip, 16, 2)

    def ring(p, d):
        return lax.rem(p + d + 4, 4)

    dev_a = [me + (ring(a, d) - a) * sa for d in (1, -1)]
    dev_b = [me + (ring(b, d) - b) * sb for d in (1, -1)]
    sib = me + 1 - 2 * core
    far = lax.rem(me + 2 * core - 1 + 64, 64)
    dev_y = me + (1 - 2 * yh) * 8

    barrier = pltpu.get_barrier_semaphore()
    peers = [sib, dev_y, *dev_a, *dev_b, far]
    for d in peers:
        pl.semaphore_signal(barrier, inc=1, device_id={"tm": d}, device_id_type=MESH)
    pl.semaphore_signal(barrier, inc=1, device_id={"segment": 1 - side}, device_id_type=MESH)

    load_tokens = pltpu.make_async_copy(tokens_hbm, tokens, in_sem.at[0])
    load_probes = pltpu.make_async_copy(probes_hbm, probes, in_sem.at[1])
    load_tokens.start()
    load_probes.start()

    k_rows, v_rows = wk[...].astype(F32), wv[...].astype(F32)
    q_rows, o_rows = wq[...].astype(F32), wo[...].astype(F32)
    mine_kv = jnp.where(flip, k_rows, v_rows)
    theirs_kv = jnp.where(flip, v_rows, k_rows)
    mine_qo = jnp.where(
        flip,
        jnp.concatenate([q_rows[:, :HALF], o_rows[:, :HALF]], 1),
        jnp.concatenate([q_rows[:, HALF:], o_rows[:, HALF:]], 1),
    )
    theirs_qo = jnp.where(
        flip,
        jnp.concatenate([q_rows[:, HALF:], o_rows[:, HALF:]], 1),
        jnp.concatenate([q_rows[:, :HALF], o_rows[:, :HALF]], 1),
    )
    stage[...] = jnp.concatenate([theirs_kv, theirs_qo], 0).astype(BF)
    pl.semaphore_wait(barrier, len(peers) + 1)
    swap = pltpu.make_async_remote_copy(
        src_ref=stage, dst_ref=got, send_sem=stage_sem.at[0], recv_sem=stage_sem.at[1],
        device_id={"tm": sib}, device_id_type=MESH,
    )
    swap.start()
    swap.wait()
    theirs = got[...].astype(F32)

    def both(mine, other):
        return jnp.where(
            flip, jnp.concatenate([mine, other], 0), jnp.concatenate([other, mine], 0)
        ).astype(BF)

    own_kv[...] = both(mine_kv, theirs[:40])
    qo = both(mine_qo, theirs[40:])
    own_q[...] = qo[:, :HALF]
    own_o[...] = qo[:, HALF:]

    def columns(s):
        if s == 0:
            return pl.ds(0, SEC)
        return pl.ds(pl.multiple_of(core * HALF, 128), HALF)

    def matrix(s, c):
        return c if s == 0 else s + 1

    def place(aa, bb):
        return jnp.where(flip, bb, aa), jnp.where(flip, aa, bb)

    def pair(s, aa, bb):
        zz, xx = place(aa, bb)
        return W.at[matrix(s, core), zz, :, xx, :, columns(s)]

    def single(s, aa, y, bb):
        zz, xx = place(aa, bb)
        return W.at[matrix(s, core), zz, y, xx, :, columns(s)]

    def send(ref, send_to, recv, device):
        pltpu.make_async_remote_copy(
            src_ref=ref, dst_ref=ref, send_sem=send_to, recv_sem=recv,
            device_id={"tm": device}, device_id_type=MESH,
        ).start()

    def await_ref(ref, sem):
        pltpu.make_async_copy(ref, ref, sem).wait()

    def send_pair(s, which, aa, bb):
        devs = dev_a if which == 0 else dev_b
        for k in range(2):
            send(pair(s, aa, bb), send_sem.at[s, which, k], pair_sem.at[s, aa, bb], devs[k])

    def send_opp(s, which, y, aa, bb):
        devs = dev_a if which == 0 else dev_b
        send(single(s, aa, y, bb), send_sem.at[s, which, y], opp_sem.at[s, y, aa, bb], devs[y])

    def to_sib(s, aa, bb):
        zz, xx = place(aa, bb)
        send(pair(s, aa, bb), send_sem.at[s, 2, 0], sib_sem.at[s, zz, xx], sib)

    def await_pair(s, aa, bb):
        await_ref(pair(s, aa, bb), pair_sem.at[s, aa, bb])

    def await_opp(s, aa, bb):
        for y in range(2):
            await_ref(single(s, aa, y, bb), opp_sem.at[s, y, aa, bb])

    def order(i):
        return jnp.where(i == 0, a, jnp.where(i == 1, ring(a, 1), jnp.where(i == 2, ring(a, -1), ring(a, 2))))

    owns = (own_kv, own_q, own_o)
    for s in range(UNITS):
        pltpu.make_async_copy(owns[s], single(s, a, yh, b), local_sem.at[s]).start()
    for s in range(UNITS):
        pltpu.make_async_copy(owns[s], single(s, a, yh, b), local_sem.at[s]).wait()
        send(single(s, a, yh, b), y_sem.at[s, 0], y_sem.at[s, 1], dev_y)
    for s in range(UNITS):
        await_ref(single(s, a, 1 - yh, b), y_sem.at[s, 1])
        send_pair(s, 0, a, b)
        if s == 0:
            send_pair(0, 1, a, b)
        to_sib(s, a, b)
    for s in range(UNITS):
        await_pair(s, ring(a, -1), b)
        send_opp(s, 0, 0, ring(a, -1), b)
        await_pair(s, ring(a, 1), b)
        send_opp(s, 0, 1, ring(a, 1), b)
        if s == 0:
            send_pair(0, 1, ring(a, 1), b)
            send_pair(0, 1, ring(a, -1), b)
        to_sib(s, ring(a, 1), b)
        to_sib(s, ring(a, -1), b)
    for s in range(UNITS):
        await_opp(s, ring(a, 2), b)
        if s == 0:
            send_pair(0, 1, ring(a, 2), b)
        to_sib(s, ring(a, 2), b)

    def start_b(s):
        for i in range(4):
            send_pair(s, 1, order(i), b)

    def pass_b(s, i):
        aa = order(i)
        await_pair(s, aa, ring(b, -1))
        send_opp(s, 1, 0, aa, ring(b, -1))
        to_sib(s, aa, ring(b, -1))
        await_pair(s, aa, ring(b, 1))
        send_opp(s, 1, 1, aa, ring(b, 1))
        to_sib(s, aa, ring(b, 1))

    def end_b(s, i):
        aa = order(i)
        await_opp(s, aa, ring(b, 2))
        to_sib(s, aa, ring(b, 2))

    def await_sib(s):
        def body(i, _):
            zz, xx = i // 4, lax.rem(i, 4)
            if s == 0:
                ref = W.at[1 - core, zz, :, xx]
            else:
                ref = W.at[s + 1, zz, :, xx, :, pl.ds(pl.multiple_of((1 - core) * HALF, 128), HALF)]
            await_ref(ref, sib_sem.at[s, zz, xx])
            return 0

        lax.fori_loop(0, 16, body, 0)

    load_tokens.wait()
    load_probes.wait()

    def norm_block(i):
        rows = pl.ds(pl.multiple_of(i * ROW_BLOCK, ROW_BLOCK), ROW_BLOCK)
        outs = norm_pair(
            tokens[rows].astype(F32), [probes[p, rows].astype(F32) for p in range(2)], gain_ref[...]
        )
        for p in range(3):
            h[p, rows] = outs[p].astype(BF)

    def first(i, _):
        lax.fori_loop(0, 4, lambda j, c: (norm_block(i * 4 + j), c)[1], 0)
        pass_b(0, i)
        return 0

    lax.fori_loop(0, 4, first, 0)
    start_b(1)
    lax.fori_loop(0, 4, lambda i, c: (end_b(0, i), c)[1], 0)
    await_sib(0)

    def project(m, n):
        cols = pl.ds(pl.multiple_of(n * 256, 256), 256)
        weight = W[m, :, :, :, :, cols].reshape(WIDTH, 256)
        return jnp.dot(
            h[...].reshape(3 * ROWS, WIDTH), weight, preferred_element_type=F32
        ).reshape(3, ROWS, 256)

    def heads_out(res, gain_ref_, n, dst, base, offset):
        for j in range(2):
            cols = pl.ds(pl.multiple_of(n * 256 + j * 128, 128), 128)
            part = res[:, :, j * 128:(j + 1) * 128]
            outs = norm_pair(part[0], [part[1], part[2]], gain_ref_[:, cols])
            for p in range(3):
                dst[base + p, pl.ds(offset, ROWS), cols] = outs[p].astype(BF)

    def halo(base, which):
        last = (core + which) == 0
        last = jnp.logical_or(last, (core + which) == 2)
        src = jnp.where(last, 2 * WIN, WIN)
        dst = jnp.where(last, 0, 3 * WIN)
        device = sib if which == 0 else far
        return pltpu.make_async_remote_copy(
            src_ref=ext.at[pl.ds(base, 3), pl.ds(pl.multiple_of(src, WIN), WIN)],
            dst_ref=ext.at[pl.ds(base, 3), pl.ds(pl.multiple_of(dst, WIN), WIN)],
            send_sem=halo_send.at[base // 3, which], recv_sem=halo_recv.at[base // 3, which],
            device_id={"tm": device}, device_id_type=MESH,
        )

    def key_tile(n, _):
        heads_out(project(0, n), kgain, n, ext, 0, WIN)
        return 0

    lax.fori_loop(0, 5, key_tile, 0)
    for which in (1, 0):
        halo(0, which).start()

    def value_tile(n, _):
        res = project(1, n)
        cols = pl.ds(pl.multiple_of(n * 256, 256), 256)
        for p in range(3):
            ext[3 + p, pl.ds(WIN, ROWS), cols] = res[p].astype(BF)

        @pl.when(n < 4)
        def _():
            pass_b(1, n)

        return 0

    lax.fori_loop(0, 5, value_tile, 0)
    for which in (1, 0):
        halo(3, which).start()
    start_b(2)
    lax.fori_loop(0, 4, lambda i, c: (end_b(1, i), c)[1], 0)
    await_sib(1)

    def query_tile(n, _):
        heads_out(project(2, n), qgain, n, q, 0, 0)

        @pl.when(n < 4)
        def _():
            pass_b(2, n)

        return 0

    lax.fori_loop(0, 5, query_tile, 0)
    for base in (0, 3):
        for which in (1, 0):
            halo(base, which).wait()

    scale = 1.0 / math.sqrt(HEAD)
    u = lax.broadcasted_iota(jnp.int32, (WIN, 3 * WIN), 0)
    w = lax.broadcasted_iota(jnp.int32, (WIN, 3 * WIN), 1)
    band = (w - u >= 0) & (w - u <= 2 * WIN)
    NT = (((1,), (1,)), ((), ()))

    def attend(head, block):
        cols = pl.ds(pl.multiple_of(head * HEAD, HEAD), HEAD)
        rows = pl.ds(pl.multiple_of(block * WIN, WIN), WIN)
        keys = pl.ds(pl.multiple_of(block * WIN, WIN), 3 * WIN)
        place_ = me * ROWS - WIN + block * WIN + w
        valid = band & (place_ >= 0) & (place_ < 64 * ROWS)
        qn, dq0, dq1 = [q[p, rows, cols] for p in range(3)]
        k, dk0, dk1, v, dv0, dv1 = [ext[p, keys, cols] for p in range(6)]
        zero = jnp.zeros_like(qn)
        left = jnp.concatenate(
            [jnp.concatenate([qn, zero], 1), jnp.concatenate([dq0, qn], 1)], 0
        )
        first_ = lax.dot_general(left, jnp.concatenate([k, dk0], 1), NT, preferred_element_type=F32)
        second = lax.dot_general(
            jnp.concatenate([dq1, qn], 1), jnp.concatenate([k, dk1], 1), NT, preferred_element_type=F32
        )
        e = jnp.where(valid, jnp.exp(first_[:WIN] * scale), 0.0)
        weights = e * (1.0 / jnp.sum(e, axis=-1, keepdims=True))
        tans = []
        for ds in (first_[WIN:], second):
            ds = jnp.where(valid, ds * scale, 0.0)
            tans.append(weights * (ds - jnp.sum(weights * ds, axis=-1, keepdims=True)))
        low = weights.astype(BF)
        stack = jnp.concatenate([low, tans[0].astype(BF), tans[1].astype(BF)], 0)
        by_v = jnp.dot(stack, v, preferred_element_type=F32)
        by_dv = jnp.dot(low, jnp.concatenate([dv0, dv1], 1), preferred_element_type=F32)
        o[0, rows, cols] = by_v[:WIN].astype(BF)
        o[1, rows, cols] = (by_v[WIN:2 * WIN] + by_dv[:, :HEAD]).astype(BF)
        o[2, rows, cols] = (by_v[2 * WIN:] + by_dv[:, HEAD:]).astype(BF)

    def attend_step(i, _):
        attend(i // 2, lax.rem(i, 2))

        @pl.when(i < 4)
        def _():
            end_b(2, i)

        return 0

    lax.fori_loop(0, 2 * HEADS, attend_step, 0)
    await_sib(2)

    def out_rows(p, half):
        weight = W[3, pl.ds(2 * half, 2)].reshape(SEC, SEC)
        return lax.dot_general(o[p], weight, NT, preferred_element_type=F32)

    away[...] = out_rows(0, 1 - side).astype(BF)
    give = pltpu.make_async_remote_copy(
        src_ref=away, dst_ref=share, send_sem=out_sem.at[0], recv_sem=out_sem.at[1],
        device_id={"segment": 1 - side}, device_id_type=MESH,
    )
    give.start()
    near[...] = out_rows(0, side)

    dens[...] = jnp.zeros_like(dens)

    def trace_step(i, _):
        p, half = i // 2, lax.rem(i, 2)
        dy = out_rows(1 + p, half)
        prod = dy * probes[p, :, pl.ds(pl.multiple_of(half * SEC, SEC), SEC)].astype(F32)
        total = prod[:, :128]
        for j in range(1, SEC // 128):
            total = total + prod[:, j * 128:(j + 1) * 128]
        dens[...] += jnp.sum(total.T, axis=0, keepdims=True)
        return 0

    lax.fori_loop(0, 4, trace_step, 0)
    give_dens = pltpu.make_async_remote_copy(
        src_ref=dens, dst_ref=dens_in, send_sem=out_sem.at[2], recv_sem=out_sem.at[3],
        device_id={"segment": 1 - side}, device_id_type=MESH,
    )
    give_dens.start()
    give.wait()
    velocity_ref[...] = (near[...] + share[...].astype(F32)).astype(BF)
    give_dens.wait()
    density_ref[...] = (dens[...] + dens_in[...]) * (1.0 / (2 * math.sqrt(WIDTH)))

    for s in range(UNITS):
        await_ref(single(s, a, yh, b), y_sem.at[s, 0])
        for k in range(2):
            for which in range(2):
                n = 3 if which == 0 else 12
                ref = W.at[0].at[pl.ds(0, 1), 0, pl.ds(0, 3)] if n == 3 else W.at[0].at[:, 0, pl.ds(0, 3)]
                ref = ref.at[:, :, :, columns(s)]
                await_ref(ref, send_sem.at[s, which, k])
        await_ref(W.at[0].at[:, :, :, :, columns(s)], send_sem.at[s, 2, 0])


def layer(tokens, probes, norm_gain, w_query, w_key, w_value, query_gain, key_gain, w_out):
    vmem = pl.BlockSpec(memory_space=pltpu.VMEM)
    hbm = pl.BlockSpec(memory_space=pl.ANY)
    V, D, R = pltpu.VMEM, pltpu.SemaphoreType.DMA, None
    velocity, density = pl.pallas_call(
        kernel,
        out_shape=(
            jax.ShapeDtypeStruct((ROWS, SEC), BF),
            jax.ShapeDtypeStruct((8, ROWS), F32),
        ),
        in_specs=[hbm, hbm] + [vmem] * 7,
        out_specs=(vmem, vmem),
        scratch_shapes=[
            V((4, 4, 2, 4, PIECE, SEC), BF),
            V((ROWS, WIDTH), BF),
            V((2, ROWS, WIDTH), jnp.int32),
            V((3, ROWS, WIDTH), BF),
            V((6, ROWS + 2 * WIN, SEC), BF),
            V((3, ROWS, SEC), BF),
            V((3, ROWS, SEC), BF),
            V((ROWS, SEC), F32),
            V((ROWS, SEC), BF),
            V((ROWS, SEC), BF),
            V((8, ROWS), F32),
            V((8, ROWS), F32),
            V((PIECE, SEC), BF),
            V((PIECE, HALF), BF),
            V((PIECE, HALF), BF),
            V((PIECE, SEC), BF),
            V((PIECE, SEC), BF),
            D((2,)), D((2,)), D((UNITS,)), D((UNITS, 2)), D((UNITS, 3, 2)),
            D((UNITS, 4, 4)), D((UNITS, 2, 4, 4)), D((UNITS, 4, 4)),
            D((2, 2)), D((2, 2)), D((4,)),
        ],
        compiler_params=pltpu.CompilerParams(
            collective_id=0, has_side_effects=True, vmem_limit_bytes=60 * 2**20
        ),
    )(
        tokens, probes, norm_gain.reshape(1, -1), w_query, w_key, w_value, w_out,
        query_gain.reshape(1, -1), key_gain.reshape(1, -1),
    )
    return velocity, density[0]


def solution(mesh):
    placed = (
        P("tm", None),
        P(None, "tm", None),
        P(),
        P("tm", "segment"),
        P("tm", "segment"),
        P("tm", "segment"),
        P("segment"),
        P("segment"),
        P("tm", "segment"),
    )
    return jax.shard_map(
        layer, mesh=mesh, in_specs=placed, out_specs=(P("tm", "segment"), P("tm")), check_vma=False
    )
```

time: 437 us -> 148 us (0.34); the launches traced: 430 us -> 148 us
  waiting for transfers between devices: 233 us -> 0 us
  Pallas kernels: 0 us -> 140 us
  matrix products: 66.1 us -> 0 us
  local copies, waits for them, and re-layouts: 64.1 us -> 7.11 us
  other arithmetic: 42.9 us -> 0 us
  between operations: 14.8 us -> 0.64 us
  starting transfers between devices: 5.74 us -> 0 us
    all_gather x4 -> x0, waiting for transfers between devices: 183 us -> none  [the longest x1 70.5 us: shards(): lax.all_gather(w_key, 'tm', axis=0, tiled=True)]
    pallas_call x0 -> x1, Pallas kernels: none -> 140 us  [layer(): pl.pallas_call(kernel, out_shape=(jax.ShapeDtypeStruct((ROWS, SEC), BF),...]
    dot_general x10 -> x0, matrix products: 66.1 us -> none  [the longest x3 27.6 us: add_rows(): return jnp.dot(rows_all, piece, preferred_element_type=jnp.float32)]
    reduce_scatter x1 -> x0, waiting for transfers between devices: 46.6 us -> none  [shards(): lax.psum_scatter(terms.astype(jnp.bfloat16), 'segment', scatter_dimension...]
    slice x16 -> x1, local copies, waits for them, and re-layouts: 33.2 us -> 1.26 us  [layer(): return (velocity, density[0])]
    convert_element_type x4 -> x0, other arithmetic: 13.4 us -> none  [the longest x2 6.39 us: norm_heads(): return (normal.astype(jnp.bfloat16), normal_tan.astype(jnp.bfloat16))]
    concatenate x3 -> x0, local copies, waits for them, and re-layouts: 13 us -> none  [the longest x1 10.7 us: extended(): block = jnp.concatenate([low, block, high], axis=dim)]
    reduce_sum x7 -> x0, other arithmetic: 11 us -> none  [the longest x3 6.85 us: norm_pair(): inner = jnp.mean(value * tangent, axis=-1, keepdims=True)]
  transfers between devices with their start and end apart: 7 -> 0, of which waited for: 4 -> 0; matrix products, arithmetic and copies ran while one was open for 36% -> 0% of each run, Pallas kernels for 0% -> 0%
where the time goes in v2:
time: 148 us
  Pallas kernels  140 us (95%)
  local copies, waits for them, and re-layouts  7.11 us (5%)
    pallas_call x1, Pallas kernels, layer(): pl.pallas_call(kernel, out_shape=(jax.ShapeDtypeStruct((ROWS, SEC), BF),...  140 us

profile of v2, /device:TPU:1, one launch (start us, length us, event | category | flops | bytes accessed | tf_op | source)
XLA Modules:
  0.0 148.1 jit_solution(7241393811395053980)
XLA Ops:
  0.6 1.3 reshape.14.qgain
  1.9 1.3 reshape.15.kgain
  3.2 1.3 reshape.13.gain_ref
  4.5 140.3 %shard_map.104 = (bf16[256,1280]{1,0:T(8,128)(2,1)}, f32[8,256]{1,0:T(8,128)}) custom-call(bf16[256,2560]{1,0:T(8,128)(2,1)} %tokens_hbm.1, s32[2,256,2560]{2,1,0:T(8,128)} %probes_hbm.1, f32[1,2560]{1,0:T(1,128)} %reshape.13.gain_ref, bf16[40,1280]{1,0:T(8,128)(2,1)} %wq.1, bf16[40,1280]{1,0:T(8,128)(2,1)} %wk.1, bf16[40,1280]{1,0:T(8,128)(2,1)} %wv.1, ...), custom_call_target="tpu_custom_call" | custom-call | tf_op jit(solution)/shard_map/pallas_call | solution.py:408
  144.9 1.3 slice.3
  146.1 2.0 %copy.12 = bf16[256,1280]{1,0:T(8,128)(2,1)} copy(bf16[256,1280]{1,0:T(8,128)(2,1)} %get-tuple-element.8) | data formatting | bytes 1310720

commit v3 on v2

v3 whole, which is shorter than its diff:
```python
import math

import jax
import jax.numpy as jnp
from jax import lax
from jax.experimental import pallas as pl
from jax.experimental.pallas import tpu as pltpu
from jax.sharding import PartitionSpec as P

MESH = pl.DeviceIdType.MESH
HEAD = 128
WIN = 128
EPS = 1e-06
BF = jnp.bfloat16
F32 = jnp.float32

ROWS = 256
WIDTH = 2560
SEC = 1280
HALF = 640
PIECE = 80
HEADS = 10
ROW_BLOCK = 16

UNITS = 4


def norm_pair(value, tangents, gain):
    factor = lax.rsqrt(jnp.mean(value * value, axis=-1, keepdims=True) + EPS)
    cube = factor * factor * factor
    outs = [value * factor * gain]
    for tangent in tangents:
        inner = jnp.mean(value * tangent, axis=-1, keepdims=True)
        outs.append((tangent * factor - value * (cube * inner)) * gain)
    return outs


def kernel(
    tokens_hbm, probes_hbm, gain_ref, wq, wk, wv, wo, qgain, kgain,
    velocity_ref, density_ref,
    W, tokens, probes, h, ext, q, o, near, away, share, dens, dens_in,
    own, stage, got,
    in_sem, stage_sem, local_sem, y_sem, send_sem, pair_sem, opp_sem, sib_sem, halo_send, halo_recv, out_sem,
):
    me = lax.axis_index("tm")
    side = lax.axis_index("segment")
    core = lax.rem(me, 2)
    x = lax.rem(me // 2, 4)
    yh = lax.rem(me // 8, 2)
    z = me // 16
    flip = core == 0

    def ring(p, d):
        return lax.rem(p + d + 4, 4)

    dev_x = [me + (ring(x, d) - x) * 2 for d in (1, -1)]
    dev_z = [me + (ring(z, d) - z) * 16 for d in (1, -1)]
    by_core = (
        jnp.where(flip, x, z),
        jnp.where(flip, z, x),
        [jnp.where(flip, i, j) for i, j in zip(dev_x, dev_z)],
        [jnp.where(flip, j, i) for i, j in zip(dev_x, dev_z)],
    )
    A, B, DEV_A, DEV_B = zip(*[by_core] * UNITS)
    sib = me + 1 - 2 * core
    far = lax.rem(me + 2 * core - 1 + 64, 64)
    dev_y = me + (1 - 2 * yh) * 8

    barrier = pltpu.get_barrier_semaphore()
    peers = [sib, dev_y, *dev_x, *dev_z, far]
    for d in peers:
        pl.semaphore_signal(barrier, inc=1, device_id={"tm": d}, device_id_type=MESH)
    pl.semaphore_signal(barrier, inc=1, device_id={"segment": 1 - side}, device_id_type=MESH)

    load_tokens = pltpu.make_async_copy(tokens_hbm, tokens, in_sem.at[0])
    load_probes = pltpu.make_async_copy(probes_hbm, probes, in_sem.at[1])
    load_tokens.start()
    load_probes.start()

    k_rows, v_rows = wk[...].astype(F32), wv[...].astype(F32)
    q_rows, o_rows = wq[...].astype(F32), wo[...].astype(F32)
    def halves(one, two):
        low = jnp.concatenate([one[:, :HALF], two[:, :HALF]], 1)
        high = jnp.concatenate([one[:, HALF:], two[:, HALF:]], 1)
        return jnp.where(flip, low, high), jnp.where(flip, high, low)

    mine_kv, theirs_kv = halves(k_rows, v_rows)
    mine_qo, theirs_qo = halves(q_rows, o_rows)
    stage[...] = jnp.concatenate([theirs_kv, theirs_qo], 0).astype(BF)
    pl.semaphore_wait(barrier, len(peers) + 1)
    swap = pltpu.make_async_remote_copy(
        src_ref=stage, dst_ref=got, send_sem=stage_sem.at[0], recv_sem=stage_sem.at[1],
        device_id={"tm": sib}, device_id_type=MESH,
    )
    swap.start()
    swap.wait()
    theirs = got[...].astype(F32)

    def both(mine, other):
        return jnp.where(
            flip, jnp.concatenate([mine, other], 0), jnp.concatenate([other, mine], 0)
        ).astype(BF)

    kv = both(mine_kv, theirs[:40])
    qo = both(mine_qo, theirs[40:])
    own[0] = kv[:, :HALF]
    own[1] = kv[:, HALF:]
    own[2] = qo[:, :HALF]
    own[3] = qo[:, HALF:]
    my_cols = pl.ds(pl.multiple_of(core * HALF, 128), HALF)
    sib_cols = pl.ds(pl.multiple_of((1 - core) * HALF, 128), HALF)

    def place(s, aa, bb):
        return jnp.where(flip, bb, aa), jnp.where(flip, aa, bb)

    def pair(s, aa, bb):
        zz, xx = place(s, aa, bb)
        return W.at[s, zz, :, xx, :, my_cols]

    def single(s, aa, y, bb):
        zz, xx = place(s, aa, bb)
        return W.at[s, zz, y, xx, :, my_cols]

    def send(ref, send_to, recv, device):
        pltpu.make_async_remote_copy(
            src_ref=ref, dst_ref=ref, send_sem=send_to, recv_sem=recv,
            device_id={"tm": device}, device_id_type=MESH,
        ).start()

    def await_ref(ref, sem):
        pltpu.make_async_copy(ref, ref, sem).wait()

    def send_pair(s, which, aa, bb):
        devs = DEV_A[s] if which == 0 else DEV_B[s]
        for k in range(2):
            send(pair(s, aa, bb), send_sem.at[s, which, k], pair_sem.at[s, aa, bb], devs[k])

    def send_single(s, which, y):
        devs = DEV_A[s] if which == 0 else DEV_B[s]
        for k in range(2):
            send(single(s, A[s], y, B[s]), send_sem.at[s, which, k], pair_sem.at[s, A[s], B[s]], devs[k])

    def send_opp(s, which, y, aa, bb):
        devs = DEV_A[s] if which == 0 else DEV_B[s]
        send(single(s, aa, y, bb), send_sem.at[s, which, y], opp_sem.at[s, y, aa, bb], devs[y])

    def to_sib(s, aa, bb):
        zz, xx = place(s, aa, bb)
        send(pair(s, aa, bb), send_sem.at[s, 2, 0], sib_sem.at[s, zz, xx], sib)

    def await_pair(s, aa, bb):
        await_ref(pair(s, aa, bb), pair_sem.at[s, aa, bb])

    def await_opp(s, aa, bb):
        for y in range(2):
            await_ref(single(s, aa, y, bb), opp_sem.at[s, y, aa, bb])

    def order(s, i):
        a = A[s]
        return jnp.where(i == 0, a, jnp.where(i == 1, ring(a, 1), jnp.where(i == 2, ring(a, -1), ring(a, 2))))

    for s in range(UNITS):
        pltpu.make_async_copy(own.at[s], single(s, A[s], yh, B[s]), local_sem.at[s]).start()
    for s in range(UNITS):
        pltpu.make_async_copy(own.at[s], single(s, A[s], yh, B[s]), local_sem.at[s]).wait()
        send(single(s, A[s], yh, B[s]), y_sem.at[s, 0], y_sem.at[s, 1], dev_y)
        send_single(s, 0, yh)
        if s == 0:
            send_single(0, 1, yh)
    load_tokens.wait()
    load_probes.wait()

    def norm_block(i):
        rows = pl.ds(pl.multiple_of(i * ROW_BLOCK, ROW_BLOCK), ROW_BLOCK)
        outs = norm_pair(
            tokens[rows].astype(F32), [probes[p, rows].astype(F32) for p in range(2)], gain_ref[...].reshape(1, WIDTH)
        )
        for p in range(3):
            h[p, rows] = outs[p].astype(BF)

    lax.fori_loop(0, ROWS // ROW_BLOCK, lambda i, c: (norm_block(i), c)[1], 0)
    part = pl.ds(pl.multiple_of(side * SEC, SEC), SEC)
    outer = pltpu.make_async_remote_copy(
        src_ref=h.at[:, pl.ds(pl.multiple_of(core * WIN, WIN), WIN), part],
        dst_ref=h.at[:, pl.ds(ROWS, WIN), part],
        send_sem=halo_send.at[2], recv_sem=halo_recv.at[2], device_id={"tm": far}, device_id_type=MESH,
    )
    relay = pltpu.make_async_remote_copy(
        src_ref=h.at[:, pl.ds(ROWS, WIN), part], dst_ref=h.at[:, pl.ds(ROWS, WIN), part],
        send_sem=halo_send.at[3], recv_sem=halo_recv.at[3], device_id={"segment": 1 - side}, device_id_type=MESH,
    )
    outer.start()

    for s in range(UNITS):
        await_ref(single(s, A[s], 1 - yh, B[s]), y_sem.at[s, 1])
        send_single(s, 0, 1 - yh)
        if s == 0:
            send_single(0, 1, 1 - yh)
        to_sib(s, A[s], B[s])
    for s in range(UNITS):
        a, b = A[s], B[s]
        await_pair(s, ring(a, -1), b)
        send_opp(s, 0, 0, ring(a, -1), b)
        await_pair(s, ring(a, 1), b)
        send_opp(s, 0, 1, ring(a, 1), b)
        if s == 0:
            send_pair(0, 1, ring(a, 1), b)
            send_pair(0, 1, ring(a, -1), b)
        to_sib(s, ring(a, 1), b)
        to_sib(s, ring(a, -1), b)
    for s in range(UNITS):
        a, b = A[s], B[s]
        await_opp(s, ring(a, 2), b)
        if s == 0:
            send_pair(0, 1, ring(a, 2), b)
        to_sib(s, ring(a, 2), b)

    def start_b(s):
        for i in range(4):
            send_pair(s, 1, order(s, i), B[s])

    def pass_b(s, i):
        aa, b = order(s, i), B[s]
        await_pair(s, aa, ring(b, -1))
        send_opp(s, 1, 0, aa, ring(b, -1))
        to_sib(s, aa, ring(b, -1))
        await_pair(s, aa, ring(b, 1))
        send_opp(s, 1, 1, aa, ring(b, 1))
        to_sib(s, aa, ring(b, 1))

    def end_b(s, i):
        aa, b = order(s, i), B[s]
        await_opp(s, aa, ring(b, 2))
        to_sib(s, aa, ring(b, 2))

    def await_sib(s):
        def body(i, _):
            zz, xx = i // 4, lax.rem(i, 4)
            await_ref(W.at[s, zz, :, xx, :, sib_cols], sib_sem.at[s, zz, xx])
            return 0

        lax.fori_loop(0, 16, body, 0)

    def first(i, _):
        pass_b(0, i)
        return 0

    lax.fori_loop(0, 4, first, 0)
    start_b(1)
    outer.wait()
    relay.start()
    lax.fori_loop(0, 4, lambda i, c: (end_b(0, i), c)[1], 0)
    await_sib(0)

    def project(m, n, rows):
        cols = pl.ds(pl.multiple_of(n * 256, 256), 256)
        weight = W[m, :, :, :, :, cols].reshape(WIDTH, 256)
        left = h[:, :rows].reshape(3 * rows, WIDTH)
        return jnp.dot(left, weight, preferred_element_type=F32).reshape(3, rows, 256)

    edge = pl.ds(pl.multiple_of(core * (ROWS + WIN), WIN), WIN)

    def to_ext(p, cols, rows):
        ext[p, pl.ds(WIN, ROWS), cols] = rows[:ROWS].astype(BF)
        ext[p, edge, cols] = rows[ROWS:].astype(BF)

    def to_q(p, cols, rows):
        q[p, :, cols] = rows.astype(BF)

    def heads_out(res, gain_ref_, n, write):
        for j in range(2):
            cols = pl.ds(pl.multiple_of(n * 256 + j * 128, 128), 128)
            part = res[:, :, j * 128:(j + 1) * 128]
            outs = norm_pair(part[0], [part[1], part[2]], gain_ref_[cols].reshape(1, 128))
            for p in range(3):
                write(p, cols, outs[p])

    def halo(base):
        return pltpu.make_async_remote_copy(
            src_ref=ext.at[pl.ds(base, 3), pl.ds(pl.multiple_of((2 - core) * WIN, WIN), WIN)],
            dst_ref=ext.at[pl.ds(base, 3), pl.ds(pl.multiple_of(core * (ROWS + WIN), WIN), WIN)],
            send_sem=halo_send.at[base // 3], recv_sem=halo_recv.at[base // 3],
            device_id={"tm": sib}, device_id_type=MESH,
        )

    def key_tile(n, _):
        heads_out(project(0, n, ROWS + WIN), kgain, n, to_ext)

        @pl.when(n > 0)
        def _():
            pass_b(1, n - 1)

        return 0

    relay.wait()
    lax.fori_loop(0, 5, key_tile, 0)
    halo(0).start()
    start_b(2)
    lax.fori_loop(0, 4, lambda i, c: (end_b(1, i), c)[1], 0)
    await_sib(1)

    def value_tile(n, _):
        @pl.when(n > 0)
        def _():
            pass_b(2, n - 1)

        res = project(1, n, ROWS + WIN)
        cols = pl.ds(pl.multiple_of(n * 256, 256), 256)
        for p in range(3):
            to_ext(3 + p, cols, res[p])
        return 0

    lax.fori_loop(0, 5, value_tile, 0)
    start_b(3)
    halo(3).start()
    lax.fori_loop(0, 4, lambda i, c: (end_b(2, i), c)[1], 0)
    await_sib(2)

    def query_tile(n, _):
        @pl.when(n < 4)
        def _():
            pass_b(3, n)

        heads_out(project(2, n, ROWS), qgain, n, to_q)
        return 0

    lax.fori_loop(0, 5, query_tile, 0)
    halo(0).wait()
    halo(3).wait()

    scale = 1.0 / math.sqrt(HEAD)
    u = lax.broadcasted_iota(jnp.int32, (WIN, 3 * WIN), 0)
    w = lax.broadcasted_iota(jnp.int32, (WIN, 3 * WIN), 1)
    band = (w - u >= 0) & (w - u <= 2 * WIN)
    NT = (((1,), (1,)), ((), ()))

    def attend(head, block):
        cols = pl.ds(pl.multiple_of(head * HEAD, HEAD), HEAD)
        rows = pl.ds(pl.multiple_of(block * WIN, WIN), WIN)
        keys = pl.ds(pl.multiple_of(block * WIN, WIN), 3 * WIN)
        place_ = me * ROWS - WIN + block * WIN + w
        valid = band & (place_ >= 0) & (place_ < 64 * ROWS)
        qn, dq0, dq1 = [q[p, rows, cols] for p in range(3)]
        k, dk0, dk1, v, dv0, dv1 = [ext[p, keys, cols] for p in range(6)]
        zero = jnp.zeros_like(qn)
        left = jnp.concatenate(
            [jnp.concatenate([qn, zero], 1), jnp.concatenate([dq0, qn], 1)], 0
        )
        first_ = lax.dot_general(left, jnp.concatenate([k, dk0], 1), NT, preferred_element_type=F32)
        second = lax.dot_general(
            jnp.concatenate([dq1, qn], 1), jnp.concatenate([k, dk1], 1), NT, preferred_element_type=F32
        )
        e = jnp.where(valid, jnp.exp(first_[:WIN] * scale), 0.0)
        weights = e * (1.0 / jnp.sum(e, axis=-1, keepdims=True))
        tans = []
        for ds in (first_[WIN:], second):
            ds = jnp.where(valid, ds * scale, 0.0)
            tans.append(weights * (ds - jnp.sum(weights * ds, axis=-1, keepdims=True)))
        low = weights.astype(BF)
        stack = jnp.concatenate([low, tans[0].astype(BF), tans[1].astype(BF)], 0)
        by_v = jnp.dot(stack, v, preferred_element_type=F32)
        by_dv = jnp.dot(low, jnp.concatenate([dv0, dv1], 1), preferred_element_type=F32)
        o[0, rows, cols] = by_v[:WIN].astype(BF)
        o[1, rows, cols] = (by_v[WIN:2 * WIN] + by_dv[:, :HEAD]).astype(BF)
        o[2, rows, cols] = (by_v[2 * WIN:] + by_dv[:, HEAD:]).astype(BF)

    def give(block):
        return pltpu.make_async_remote_copy(
            src_ref=away.at[block], dst_ref=share.at[block],
            send_sem=out_sem.at[block, 0], recv_sem=out_sem.at[block, 1],
            device_id={"segment": 1 - side}, device_id_type=MESH,
        )

    def out_half(left, half):
        weight = W[3, pl.ds(2 * half, 2)].reshape(SEC, SEC)
        return lax.dot_general(left, weight, NT, preferred_element_type=F32)

    def block_step(block, _):
        lax.fori_loop(0, HEADS, lambda i, c: (attend(i, block), c)[1], 0)

        @pl.when(block == 0)
        def _():
            lax.fori_loop(0, 4, lambda i, c: (end_b(3, i), c)[1], 0)
            await_sib(3)

        rows = pl.ds(pl.multiple_of(block * WIN, WIN), WIN)
        away[block] = out_half(o[0, rows], 1 - side).astype(BF)
        give(block).start()
        return 0

    lax.fori_loop(0, 2, block_step, 0)
    near[...] = out_half(o[0], side)
    dens[...] = jnp.zeros_like(dens)

    def trace_step(i, _):
        p, half = i // 2, lax.rem(i, 2)
        dy = out_half(o[1 + p], half)
        prod = dy * probes[p, :, pl.ds(pl.multiple_of(half * SEC, SEC), SEC)].astype(F32)
        total = prod[:, :128]
        for j in range(1, SEC // 128):
            total = total + prod[:, j * 128:(j + 1) * 128]
        dens[...] += jnp.sum(total.T, axis=0, keepdims=True)
        return 0

    lax.fori_loop(0, 4, trace_step, 0)
    give_dens = pltpu.make_async_remote_copy(
        src_ref=dens, dst_ref=dens_in, send_sem=out_sem.at[2, 0], recv_sem=out_sem.at[2, 1],
        device_id={"segment": 1 - side}, device_id_type=MESH,
    )
    give_dens.start()
    for block in range(2):
        give(block).wait()
        rows = pl.ds(block * WIN, WIN)
        velocity_ref[rows] = (near[rows] + share[block].astype(F32)).astype(BF)
    give_dens.wait()
    density_ref[...] = (dens[0] + dens_in[0]) * (1.0 / (2 * math.sqrt(WIDTH)))

    for s in range(UNITS):
        await_ref(single(s, A[s], yh, B[s]), y_sem.at[s, 0])
        for k in range(2):
            for which in range(2):
                n = 3 if which == 0 else 12
                ref = W.at[0].at[pl.ds(0, 1), 0, pl.ds(0, 3)] if n == 3 else W.at[0].at[:, 0, pl.ds(0, 3)]
                ref = ref.at[:, :, :, my_cols]
                await_ref(ref, send_sem.at[s, which, k])
        await_ref(W.at[0].at[:, :, :, :, my_cols], send_sem.at[s, 2, 0])


def layer(tokens, probes, norm_gain, w_query, w_key, w_value, query_gain, key_gain, w_out):
    vmem = pl.BlockSpec(memory_space=pltpu.VMEM)
    hbm = pl.BlockSpec(memory_space=pl.ANY)
    V, D, R = pltpu.VMEM, pltpu.SemaphoreType.DMA, None
    velocity, density = pl.pallas_call(
        kernel,
        out_shape=(
            jax.ShapeDtypeStruct((ROWS, SEC), BF),
            jax.ShapeDtypeStruct((ROWS,), F32),
        ),
        in_specs=[hbm, hbm] + [vmem] * 7,
        out_specs=(vmem, vmem),
        scratch_shapes=[
            V((4, 4, 2, 4, PIECE, SEC), BF),
            V((ROWS, WIDTH), BF),
            V((2, ROWS, WIDTH), jnp.int32),
            V((3, ROWS + WIN, WIDTH), BF),
            V((6, ROWS + 2 * WIN, SEC), BF),
            V((3, ROWS, SEC), BF),
            V((3, ROWS, SEC), BF),
            V((ROWS, SEC), F32),
            V((2, WIN, SEC), BF),
            V((2, WIN, SEC), BF),
            V((8, ROWS), F32),
            V((8, ROWS), F32),
            V((UNITS, PIECE, HALF), BF),
            V((PIECE, SEC), BF),
            V((PIECE, SEC), BF),
            D((2,)), D((2,)), D((UNITS,)), D((UNITS, 2)), D((UNITS, 3, 2)),
            D((UNITS, 4, 4)), D((UNITS, 2, 4, 4)), D((UNITS, 4, 4)),
            D((4,)), D((4,)), D((3, 2)),
        ],
        compiler_params=pltpu.CompilerParams(
            collective_id=0, has_side_effects=True, vmem_limit_bytes=60 * 2**20
        ),
    )(
        tokens, probes, norm_gain, w_query, w_key, w_value, w_out,
        query_gain, key_gain,
    )
    return velocity, density


def solution(mesh):
    placed = (
        P("tm", None),
        P(None, "tm", None),
        P(),
        P("tm", "segment"),
        P("tm", "segment"),
        P("tm", "segment"),
        P("segment"),
        P("segment"),
        P("tm", "segment"),
    )
    return jax.shard_map(
        layer, mesh=mesh, in_specs=placed, out_specs=(P("tm", "segment"), P("tm")), check_vma=False
    )
```

time: 148 us -> 141 us (0.953)
  local copies, waits for them, and re-layouts: 7.11 us -> 3.19 us
  Pallas kernels: 140 us -> 137 us
    reshape x3 -> x0, local copies, waits for them, and re-layouts: 3.89 us -> none  [the longest x1 1.31 us: layer(): norm_gain.reshape(1, -1)]
    pallas_call x1, Pallas kernels: 140 us -> 137 us  [layer(): pl.pallas_call(kernel, out_shape=(jax.ShapeDtypeStruct((ROWS, SEC), BF),...]
    unnamed x1 -> x2, local copies, waits for them, and re-layouts: 1.96 us -> 3.19 us
where the time goes in v3:
time: 141 us
  Pallas kernels  137 us (97%)
  local copies, waits for them, and re-layouts  3.19 us (2%)
    pallas_call x1, Pallas kernels, layer(): pl.pallas_call(kernel, out_shape=(jax.ShapeDtypeStruct((ROWS, SEC), BF),...  137 us
    unnamed x2, local copies, waits for them, and re-layouts  3.19 us

profile of v3, /device:TPU:1, one launch (start us, length us, event | category | flops | bytes accessed | tf_op | source)
XLA Modules:
  0.0 141.0 jit_solution(14114141265405375742)
XLA Ops:
  0.6 137.2 %shard_map.104 = (bf16[256,1280]{1,0:T(8,128)(2,1)}, f32[256]{0:T(256)}) custom-call(bf16[256,2560]{1,0:T(8,128)(2,1)} %tokens_hbm.1, s32[2,256,2560]{2,1,0:T(8,128)} %probes_hbm.1, f32[2560]{0:T(1024)} %gain_ref.1, bf16[40,1280]{1,0:T(8,128)(2,1)} %wq.1, bf16[40,1280]{1,0:T(8,128)(2,1)} %wk.1, bf16[40,1280]{1,0:T(8,128)(2,1)} %wv.1, bf16[40,1280]{1,0:T(8,128)(2,1)} %wo.1, ...), custom_call_target="tpu_custom_call" | custom-call | tf_op jit(solution)/shard_map/pallas_call | solution.py:433
  137.8 2.0 %copy.13 = bf16[256,1280]{1,0:T(8,128)(2,1)} copy(bf16[256,1280]{1,0:T(8,128)(2,1)} %get-tuple-element.4) | data formatting | bytes 1310720
  139.8 1.2 copy.14

commit v4 on v3

--- a/solution.py
+++ b/solution.py
@@ -247,22 +247,22 @@
 
     lax.fori_loop(0, 4, first, 0)
     start_b(1)
-    outer.wait()
-    relay.start()
     lax.fori_loop(0, 4, lambda i, c: (end_b(0, i), c)[1], 0)
     await_sib(0)
 
-    def project(m, n, rows):
+    def project(m, n, first_row, rows):
         cols = pl.ds(pl.multiple_of(n * 256, 256), 256)
         weight = W[m, :, :, :, :, cols].reshape(WIDTH, 256)
-        left = h[:, :rows].reshape(3 * rows, WIDTH)
+        left = h[:, first_row:first_row + rows].reshape(3 * rows, WIDTH)
         return jnp.dot(left, weight, preferred_element_type=F32).reshape(3, rows, 256)
 
     edge = pl.ds(pl.multiple_of(core * (ROWS + WIN), WIN), WIN)
 
     def to_ext(p, cols, rows):
-        ext[p, pl.ds(WIN, ROWS), cols] = rows[:ROWS].astype(BF)
-        ext[p, edge, cols] = rows[ROWS:].astype(BF)
+        ext[p, pl.ds(WIN, ROWS), cols] = rows.astype(BF)
+
+    def to_edge(p, cols, rows):
+        ext[p, edge, cols] = rows.astype(BF)
 
     def to_q(p, cols, rows):
         q[p, :, cols] = rows.astype(BF)
@@ -284,7 +284,7 @@
         )
 
     def key_tile(n, _):
-        heads_out(project(0, n, ROWS + WIN), kgain, n, to_ext)
+        heads_out(project(0, n, 0, ROWS), kgain, n, to_ext)
 
         @pl.when(n > 0)
         def _():
@@ -292,7 +292,8 @@
 
         return 0
 
-    relay.wait()
+    outer.wait()
+    relay.start()
     lax.fori_loop(0, 5, key_tile, 0)
     halo(0).start()
     start_b(2)
@@ -304,7 +305,7 @@
         def _():
             pass_b(2, n - 1)
 
-        res = project(1, n, ROWS + WIN)
+        res = project(1, n, 0, ROWS)
         cols = pl.ds(pl.multiple_of(n * 256, 256), 256)
         for p in range(3):
             to_ext(3 + p, cols, res[p])
@@ -313,6 +314,17 @@
     lax.fori_loop(0, 5, value_tile, 0)
     start_b(3)
     halo(3).start()
+
+    def edge_tile(n, _):
+        heads_out(project(0, n, ROWS, WIN), kgain, n, to_edge)
+        res = project(1, n, ROWS, WIN)
+        cols = pl.ds(pl.multiple_of(n * 256, 256), 256)
+        for p in range(3):
+            to_edge(3 + p, cols, res[p])
+        return 0
+
+    relay.wait()
+    lax.fori_loop(0, 5, edge_tile, 0)
     lax.fori_loop(0, 4, lambda i, c: (end_b(2, i), c)[1], 0)
     await_sib(2)
 
@@ -321,7 +333,7 @@
         def _():
             pass_b(3, n)
 
-        heads_out(project(2, n, ROWS), qgain, n, to_q)
+        heads_out(project(2, n, 0, ROWS), qgain, n, to_q)
         return 0
 
     lax.fori_loop(0, 5, query_tile, 0)

time: 141 us -> 129 us (0.915)
  Pallas kernels: 137 us -> 125 us
    pallas_call x1, Pallas kernels: 137 us -> 125 us  [layer(): pl.pallas_call(kernel, out_shape=(jax.ShapeDtypeStruct((ROWS, SEC), BF),...]
where the time goes in v4:
time: 129 us; the launch traced here: 128 us
  Pallas kernels  125 us (97%)
  local copies, waits for them, and re-layouts  3.19 us (2%)
    pallas_call x1, Pallas kernels, layer(): pl.pallas_call(kernel, out_shape=(jax.ShapeDtypeStruct((ROWS, SEC), BF),...  125 us
    unnamed x2, local copies, waits for them, and re-layouts  3.19 us

profile of v4, /device:TPU:1, one launch (start us, length us, event | category | flops | bytes accessed | tf_op | source)
XLA Modules:
  0.0 128.4 jit_solution(555716363723484537)
XLA Ops:
  0.6 124.6 %shard_map.104 = (bf16[256,1280]{1,0:T(8,128)(2,1)}, f32[256]{0:T(256)}) custom-call(bf16[256,2560]{1,0:T(8,128)(2,1)} %tokens_hbm.1, s32[2,256,2560]{2,1,0:T(8,128)} %probes_hbm.1, f32[2560]{0:T(1024)} %gain_ref.1, bf16[40,1280]{1,0:T(8,128)(2,1)} %wq.1, bf16[40,1280]{1,0:T(8,128)(2,1)} %wk.1, bf16[40,1280]{1,0:T(8,128)(2,1)} %wv.1, bf16[40,1280]{1,0:T(8,128)(2,1)} %wo.1, ...), custom_call_target="tpu_custom_call" | custom-call | tf_op jit(solution)/shard_map/pallas_call | solution.py:445
  125.3 2.0 %copy.13 = bf16[256,1280]{1,0:T(8,128)(2,1)} copy(bf16[256,1280]{1,0:T(8,128)(2,1)} %get-tuple-element.4) | data formatting | bytes 1310720
  127.2 1.2 copy.14

commit v5 on v4

--- a/solution.py
+++ b/solution.py
@@ -388,7 +388,7 @@
         return lax.dot_general(left, weight, NT, preferred_element_type=F32)
 
     def block_step(block, _):
-        lax.fori_loop(0, HEADS, lambda i, c: (attend(i, block), c)[1], 0)
+        lax.fori_loop(0, HEADS // 2, lambda i, c: (attend(2 * i, block), attend(2 * i + 1, block), c)[2], 0)
 
         @pl.when(block == 0)
         def _():

time: 129 us -> 128 us (level)
  no operation moved by 1% of the time
where the time goes in v5:
time: 128 us; the launch traced here: 127 us
  Pallas kernels  124 us (97%)
  local copies, waits for them, and re-layouts  3.19 us (2%)
    pallas_call x1, Pallas kernels, layer(): pl.pallas_call(kernel, out_shape=(jax.ShapeDtypeStruct((ROWS, SEC), BF),...  124 us
    unnamed x2, local copies, waits for them, and re-layouts  3.19 us

profile of v5, /device:TPU:1, one launch (start us, length us, event | category | flops | bytes accessed | tf_op | source)
XLA Modules:
  0.0 127.3 jit_solution(8531199129708100422)
XLA Ops:
  0.6 123.5 %shard_map.104 = (bf16[256,1280]{1,0:T(8,128)(2,1)}, f32[256]{0:T(256)}) custom-call(bf16[256,2560]{1,0:T(8,128)(2,1)} %tokens_hbm.1, s32[2,256,2560]{2,1,0:T(8,128)} %probes_hbm.1, f32[2560]{0:T(1024)} %gain_ref.1, bf16[40,1280]{1,0:T(8,128)(2,1)} %wq.1, bf16[40,1280]{1,0:T(8,128)(2,1)} %wk.1, bf16[40,1280]{1,0:T(8,128)(2,1)} %wv.1, bf16[40,1280]{1,0:T(8,128)(2,1)} %wo.1, ...), custom_call_target="tpu_custom_call" | custom-call | tf_op jit(solution)/shard_map/pallas_call | solution.py:445
  124.1 2.0 %copy.13 = bf16[256,1280]{1,0:T(8,128)(2,1)} copy(bf16[256,1280]{1,0:T(8,128)(2,1)} %get-tuple-element.4) | data formatting | bytes 1310720
  126.1 1.2 copy.14

commit v6 on v5

--- a/solution.py
+++ b/solution.py
@@ -388,7 +388,7 @@
         return lax.dot_general(left, weight, NT, preferred_element_type=F32)
 
     def block_step(block, _):
-        lax.fori_loop(0, HEADS // 2, lambda i, c: (attend(2 * i, block), attend(2 * i + 1, block), c)[2], 0)
+        lax.fori_loop(0, 2, lambda i, c: ([attend(5 * i + k, block) for k in range(5)], c)[1], 0)
 
         @pl.when(block == 0)
         def _():

time: 128 us -> 128 us (level)
  no operation moved by 1% of the time
where the time goes in v6:
time: 128 us; the launch traced here: 127 us
  Pallas kernels  123 us (96%)
  local copies, waits for them, and re-layouts  3.19 us (2%)
    pallas_call x1, Pallas kernels, layer(): pl.pallas_call(kernel, out_shape=(jax.ShapeDtypeStruct((ROWS, SEC), BF),...  123 us
    unnamed x2, local copies, waits for them, and re-layouts  3.19 us

profile of v6, /device:TPU:1, one launch (start us, length us, event | category | flops | bytes accessed | tf_op | source)
XLA Modules:
  0.0 126.8 jit_solution(13563959964262093643)
XLA Ops:
  0.6 123.0 %shard_map.104 = (bf16[256,1280]{1,0:T(8,128)(2,1)}, f32[256]{0:T(256)}) custom-call(bf16[256,2560]{1,0:T(8,128)(2,1)} %tokens_hbm.1, s32[2,256,2560]{2,1,0:T(8,128)} %probes_hbm.1, f32[2560]{0:T(1024)} %gain_ref.1, bf16[40,1280]{1,0:T(8,128)(2,1)} %wq.1, bf16[40,1280]{1,0:T(8,128)(2,1)} %wk.1, bf16[40,1280]{1,0:T(8,128)(2,1)} %wv.1, bf16[40,1280]{1,0:T(8,128)(2,1)} %wo.1, ...), custom_call_target="tpu_custom_call" | custom-call | tf_op jit(solution)/shard_map/pallas_call | solution.py:445
  123.7 2.0 %copy.13 = bf16[256,1280]{1,0:T(8,128)(2,1)} copy(bf16[256,1280]{1,0:T(8,128)(2,1)} %get-tuple-element.4) | data formatting | bytes 1310720
  125.6 1.2 copy.14
